TPU v7x, 32 devices: a whole 2x2x4 slice. The times are simulated.
32 devices in a mesh: row: 4 (over x, core), col: 8 (over z, y).
Axes of the slice: x: 2, y: 2, z: 4, core: 2. Of those that a mesh axis runs over, the one named last changes fastest.
Arguments:
- blocks: float32 [4, 8, 4, 128, 128], P('row', 'col')
- block_rows: int32 [4, 8, 4], P('row', 'col'), may hold values from 0 to 31, as said below
- block_cols: int32 [4, 8, 4], P('row', 'col'), may hold values from 0 to 7
- counts: int32 [4, 8], P('row', 'col'), may hold values from 2 to 4, as said below
- x_prev: float32 [8192], P('col'), may hold values from 0 to 1
- y_prev: float32 [16384], P('row'), may hold values from -6 to 6
- cost: float32 [8192], P('col'), may hold values from -6 to 6
- rhs: float32 [16384], P('row'), may hold values from -6 to 6
- upper: float32 [8192], P('col'), may hold values from 0.5 to 4
- steps: float32 [2], replicated, may hold values from 0.1 to 0.4
Outputs:
- x_new: float32 [8192], P('col')
- y_new: float32 [16384], P('row')
- stats: float32 [3], replicated
Inputs may be any that keep to these rules, and one draw needn't show every extreme that they name: `block_rows`: pairs of block row and block column may repeat within a device. `counts`: stored blocks at positions from the count on are padding and are not part of the matrix; some device holds 4 live blocks in every draw.
All inputs are finite; a program needn't handle non-finite values.
Results may differ from a plain program's by a relative error of at most 0.00011.
Values sent between devices are 32-bit elements; how exact they have to be, the bound alone decides.
No kernel may reach another device: no remote copies, remote signals or barrier semaphores. Data moves between devices by JAX's collectives and lax.ppermute only.
A program may use at most 64 MiB of HBM per device.

v0:
```python
import jax
import jax.numpy as jnp
from jax import lax
from jax.sharding import PartitionSpec as P


def shards(blocks, block_rows, block_cols, counts, x_prev, y_prev, cost, rhs, upper, steps):
    flat = blocks[0, 0]
    nbd = flat.shape[0]
    bsz = flat.shape[1]
    brow = block_rows[0, 0]
    bcol = block_cols[0, 0]
    live = (jnp.arange(nbd, dtype=jnp.int32) < counts[0, 0]).astype(jnp.float32)
    nrows = y_prev.shape[0]
    ncols = x_prev.shape[0]
    rblocks = nrows // bsz
    cblocks = ncols // bsz
    row_hot = (brow[:, None] == jnp.arange(rblocks, dtype=jnp.int32)[None, :]).astype(jnp.float32)
    col_hot = (bcol[:, None] == jnp.arange(cblocks, dtype=jnp.int32)[None, :]).astype(jnp.float32)
    row_live = row_hot * live[:, None]
    col_live = col_hot * live[:, None]
    rpeak = jnp.max(jnp.abs(flat), axis=2)
    cpeak = jnp.max(jnp.abs(flat), axis=1)
    rpeak = jnp.max(row_live[:, :, None] * rpeak[:, None, :], axis=0).reshape(-1)
    cpeak = jnp.max(col_live[:, :, None] * cpeak[:, None, :], axis=0).reshape(-1)
    rowmax = lax.pmax(rpeak, "col")
    colmax = lax.pmax(cpeak, "row")
    row_scale = 1.0 / jnp.sqrt(jnp.maximum(rowmax, 0.5))
    col_scale = 1.0 / jnp.sqrt(jnp.maximum(colmax, 0.5))

    def backward(vec):
        scaled = (vec * row_scale).reshape(rblocks, bsz)
        picked = jnp.einsum("kr,ri->ki", row_hot, scaled, precision=lax.Precision.HIGHEST)
        prod = jnp.einsum("kij,ki->kj", flat, picked, precision=lax.Precision.HIGHEST)
        partial_value = jnp.einsum(
            "kc,kj->cj", col_live, prod, precision=lax.Precision.HIGHEST
        ).reshape(-1)
        return lax.psum(partial_value, "row") * col_scale

    cost_s = col_scale * cost
    rhs_s = row_scale * rhs
    upper_s = upper / col_scale
    eta = steps[0]
    omega = steps[1]
    tau = eta / omega
    sigma = eta * omega
    grad = cost_s - backward(y_prev)
    x_new = jnp.clip(x_prev - tau * grad, 0.0, upper_s)
    delta_x = x_new - x_prev
    vecs = jnp.stack([x_new, delta_x])
    count = vecs.shape[0]
    scaled = (vecs * col_scale[None, :]).reshape(count, cblocks, bsz)
    picked = jnp.einsum("kc,vcj->vkj", col_hot, scaled, precision=lax.Precision.HIGHEST)
    prod = jnp.einsum("kij,vkj->kvi", flat, picked, precision=lax.Precision.HIGHEST)
    summed = jnp.einsum("kr,kvi->vri", row_live, prod, precision=lax.Precision.HIGHEST)
    partial_value = summed.reshape(count, nrows)
    share = nrows // lax.axis_size("col")
    start = lax.axis_index("col") * share

    def piece(vec):
        return lax.dynamic_slice_in_dim(vec, start, share)

    summed = lax.psum(partial_value, "col")
    ax_new = summed[0] * row_scale
    adx = summed[1] * row_scale
    y_new = y_prev + sigma * (rhs_s - ax_new - adx)
    rhs_piece = piece(rhs_s)
    y_new_piece = piece(y_new)
    delta_y = y_new_piece - piece(y_prev)
    adx_piece = piece(adx)
    resid = rhs_piece - piece(ax_new)
    dual_terms = jnp.stack(
        [
            jnp.sum(delta_y * delta_y),
            jnp.sum(adx_piece * adx_piece),
            jnp.sum(resid * resid),
            jnp.sum(rhs_piece * y_new_piece),
        ]
    )
    reduced = cost_s - backward(y_new)
    rshare = ncols // lax.axis_size("row")
    rstart = lax.axis_index("row") * rshare

    def row_piece(vec):
        return lax.dynamic_slice_in_dim(vec, rstart, rshare)

    dx_piece = row_piece(delta_x)
    primal_terms = jnp.stack(
        [
            jnp.sum(dx_piece * dx_piece),
            jnp.sum(row_piece(cost_s) * row_piece(x_new)),
            jnp.sum(row_piece(upper_s) * jnp.maximum(-row_piece(reduced), 0.0)),
        ]
    )
    joined = lax.psum(jnp.concatenate([primal_terms, dual_terms]), ("row", "col"))
    primal_total = joined[:3]
    dual_total = joined[3:]
    total_rows = nrows * lax.axis_size("row")
    total_cols = ncols * lax.axis_size("col")
    movement = 0.5 * omega * primal_total[0] + 0.5 / omega * dual_total[0]
    stats = jnp.stack(
        [
            jnp.sqrt(dual_total[2] / total_rows),
            (primal_total[1] - dual_total[3] + primal_total[2]) / total_cols,
            movement / jnp.sqrt(dual_total[1] * dual_total[0] + 1e-06),
        ]
    )
    return (x_new, y_new, stats)


def solution(mesh):
    placed = (
        P("row", "col", None, None, None),
        P("row", "col", None),
        P("row", "col", None),
        P("row", "col"),
        P("col"),
        P("row"),
        P("col"),
        P("row"),
        P("col"),
        P(),
    )
    return jax.shard_map(
        shards, mesh=mesh, in_specs=placed, out_specs=(P("col"), P("row"), P()), check_vma=False
    )
```

profile of v0, /device:TPU:0, one launch (start us, length us, event | category | flops | bytes accessed | tf_op | source)
XLA Modules:
  0.0 154.5 jit_solution(2279663785784154501)
XLA Ops:
  0.6 0.0 copy-start
  1.3 1.3 fusion.54
  6.6 0.7 fusion.27
  7.4 0.7 fusion.29
  8.1 1.1 fusion.7
  9.2 0.1 multiply_reduce_fusion.1
  9.3 8.3 %pmax.14 = f32[1024]{0:T(1024)S(1)} all-reduce(f32[1024]{0:T(1024)S(1)} %bitcast.78), channel_id=1, replica_groups=mesh['row'=4,'col'=8] {'row'}, use_global_device_ids=true, to_apply=%region_2.0 | all-reduce | flops 1024 | bytes 8192 | tf_op jit(solution)/shard_map/pmax | solution.py:27
  17.6 0.1 multiply_reduce_fusion
  17.7 0.0 copy-start.1
  17.7 0.0 copy-start.9
  17.7 37.4 %pmax.15 = f32[4096]{0:T(1024)S(1)} all-reduce(f32[4096]{0:T(1024)S(1)} %bitcast.73), channel_id=1, replica_groups=mesh['row'=4,'col'=8] {'col'}, use_global_device_ids=true, to_apply=%region_5.0 | all-reduce | flops 4096 | bytes 32768 | tf_op jit(solution)/shard_map/pmax | solution.py:26
  55.1 0.0 copy-done.1
  55.1 0.0 copy-done.9
  55.1 0.2 fusion.10
  55.3 0.0 copy-done
  55.3 0.3 fusion.4
  55.6 0.0 copy-start.8
  55.6 0.7 copy-done.8
  56.3 0.0 copy-start.7
  56.3 0.3 convolution_bitcast_fusion.3
  56.5 0.0 copy-start.5
  56.5 0.0 copy-start.6
  56.5 5.9 %psum.28 = f32[1024]{0:T(1024)S(1)} all-reduce(f32[1024]{0:T(1024)S(1)} %convolution_bitcast_fusion.3), channel_id=1, replica_groups=mesh['row'=4,'col'=8] {'row'}, use_global_device_ids=true, to_apply=%region_6.0 | all-reduce | flops 1024 | bytes 8192 | tf_op jit(solution)/shard_map/psum | solution.py:38
  62.4 0.0 copy-done.7
  62.4 0.0 copy-done.5
  62.4 0.0 copy-done.6
  62.4 0.0 copy-start.3
  62.5 0.8 multiply_reduce_fusion.7
  63.2 0.0 copy-done.3
  63.2 0.3 convolution_bitcast_fusion
  63.6 0.1 copy.15
  63.6 0.5 fusion.2
  64.2 0.3 convolution_bitcast_fusion.1
  64.5 33.0 %psum.29 = f32[2,4096]{1,0:T(2,128)S(1)} all-reduce(f32[2,4096]{1,0:T(2,128)S(1)} %bitcast.72), channel_id=1, replica_groups=mesh['row'=4,'col'=8] {'col'}, use_global_device_ids=true, to_apply=%region_7.8 | all-reduce | flops 8192 | bytes 65536 | tf_op jit(solution)/shard_map/psum | solution.py:63
  97.5 0.0 copy-start.4
  97.6 0.7 copy-done.4
  98.3 0.0 copy-start.2
  98.3 0.2 fusion.8
  98.5 0.3 fusion
  98.8 0.7 multiply_reduce_fusion.4
  99.5 0.0 copy-done.2
  99.5 0.7 multiply_reduce_fusion.2
  100.2 0.3 convolution_bitcast_fusion.2
  100.5 5.7 %psum.30 = f32[1024]{0:T(1024)S(1)} all-reduce(f32[1024]{0:T(1024)S(1)} %convolution_bitcast_fusion.2), channel_id=1, replica_groups=mesh['row'=4,'col'=8] {'row'}, use_global_device_ids=true, to_apply=%region_10.11 | all-reduce | flops 1024 | bytes 8192 | tf_op jit(solution)/shard_map/psum | solution.py:38
  106.2 0.7 multiply_reduce_fusion.6
  106.9 4.5 %concatenate.4 = f32[7]{0:T(128)S(1)} concatenate(f32[1]{0:T(128)} %bitcast.23, f32[1]{0:T(128)} %bitcast.24, f32[1]{0:T(128)} %bitcast.31, f32[1]{0:T(128)} %bitcast.32, f32[1]{0:T(128)} %bitcast.33, f32[1]{0:T(128)} %bitcast.34, f32[1]{0:T(128)} %bitcast.35), dimensions={0} | concatenate | bytes 56 | tf_op jit(solution)/shard_map/concatenate | solution.py:95
  111.4 36.8 %psum.31 = f32[7]{0:T(128)S(1)} all-reduce(f32[7]{0:T(128)S(1)} %concatenate.4), channel_id=1, replica_groups=mesh['row'=4,'col'=8] {'row','col'}, use_global_device_ids=true, to_apply=%region_16.17 | all-reduce | flops 7 | bytes 56 | tf_op jit(solution)/shard_map/psum | solution.py:95
  148.2 0.7 fusion.53
  153.9 0.6 pad_maximum_fusion
  (6 shorter events, 0.1 us)
Async XLA Ops:
  0.6 54.6 %copy-start = (f32[1,1,4,128,128]{4,3,2,1,0:T(8,128)S(1)}, f32[1,1,4,128,128]{4,3,2,1,0:T(8,128)}, u32[]{:S(2)}) copy-start(f32[1,1,4,128,128]{4,3,2,1,0:T(8,128)} %param.10) | copy-start | bytes 786436
  17.7 37.4 %copy-start.1 = (f32[4096]{0:T(1024)S(1)}, f32[4096]{0:T(1024)}, u32[]{:S(2)}) copy-start(f32[4096]{0:T(1024)} %param.15) | copy-start | bytes 49156
  17.7 37.4 %copy-start.9 = (s32[1,1,4]{2,1,0:T(1,128)S(1)}, s32[1,1,4]{2,1,0:T(1,128)}, u32[]{:S(2)}) copy-start(s32[1,1,4]{2,1,0:T(1,128)} %param.11) | copy-start | bytes 52
  55.6 0.7 copy-start.8
  56.3 6.2 %copy-start.7 = (f32[1024]{0:T(1024)S(1)}, f32[1024]{0:T(1024)}, u32[]{:S(2)}) copy-start(f32[1024]{0:T(1024)} %param.18) | copy-start | bytes 12292
  56.5 5.9 %copy-start.5 = (f32[1024]{0:T(1024)S(1)}, f32[1024]{0:T(1024)}, u32[]{:S(2)}) copy-start(f32[1024]{0:T(1024)} %param.16) | copy-start | bytes 12292
  56.5 5.9 %copy-start.6 = (f32[1024]{0:T(1024)S(1)}, f32[1024]{0:T(1024)}, u32[]{:S(2)}) copy-start(f32[1024]{0:T(1024)} %param.14) | copy-start | bytes 12292
  62.4 0.8 copy-start.3
  97.5 0.7 copy-start.4
  98.3 1.2 copy-start.2
where the time goes:
time: 156 us; the launch traced here: 154 us
  blocking collectives  127 us (81%)
  between operations  10.4 us (7%)
  local copies, waits for them, and re-layouts  7.97 us (5%)
  other arithmetic  6.2 us (4%)
  matrix products  2.7 us (2%)
    pmax x1, blocking collectives, shards(): rowmax = lax.pmax(rpeak, 'col')  37.4 us
    psum x1, blocking collectives, shards(): lax.psum(jnp.concatenate([primal_terms, dual_terms]), ('row', 'col'))  36.8 us
    psum x1, blocking collectives, shards(): summed = lax.psum(partial_value, 'col')  33 us
    psum x2, blocking collectives, backward(): return lax.psum(partial_value, 'row') * col_scale  11.6 us
    pmax x1, blocking collectives, shards(): colmax = lax.pmax(cpeak, 'row')  8.31 us
    concatenate x1, local copies, waits for them, and re-layouts, shards(): jnp.concatenate([primal_terms, dual_terms])  4.46 us

commit v1 on v0

v1 whole, which is shorter than its diff:
```python
import functools

import jax
import jax.numpy as jnp
from jax import lax
from jax.experimental import pallas as pl
from jax.experimental.pallas import tpu as pltpu
from jax.sharding import PartitionSpec as P

F32 = jnp.float32
VMEM = pl.BlockSpec(memory_space=pltpu.VMEM)
SMEM = pl.BlockSpec(memory_space=pltpu.SMEM)
LIMIT = 40 * 1024 * 1024


def up(n, m):
    return -(-n // m) * m


def iota(shape, dim):
    return lax.broadcasted_iota(jnp.int32, shape, dim)


def rows_of(rows, bsz):
    lane = iota((bsz, bsz), 1)
    cols = jnp.zeros((bsz, bsz), F32)
    for k, col in enumerate(rows):
        cols = jnp.where(lane == k, col, cols)
    return cols.T


def peaks_kernel(nbd, blocks, y, rhs, brow, bcol, count, p1, bulk):
    bsz = blocks.shape[1]
    hp = p1.shape[1]
    rb = y.shape[0]
    peaks = []
    for k in range(nbd):
        a = blocks[k * bsz : (k + 1) * bsz, :]
        bulk[k * bsz : (k + 1) * bsz, :] = a
        peaks.append(jnp.max(jnp.abs(a), axis=1, keepdims=True))
    rows = rows_of(peaks, bsz)[:hp]
    sub = iota((hp, bsz), 0)
    base = nbd * bsz
    bulk[base : base + rb, :] = y[...]
    bulk[base + rb : base + 2 * rb, :] = rhs[...]
    ch = bulk.shape[0] - base - 2 * rb
    csub = iota((ch, bsz), 0)
    cols = jnp.zeros((ch, bsz), F32)
    for k in range(nbd):
        code = jnp.where(k < count[0], brow[k], -1).astype(F32)
        rows = jnp.where(sub == nbd + k, code, rows)
        cols = jnp.where(csub == k, bcol[k].astype(F32), cols)
    bulk[base + 2 * rb :, :] = cols
    p1[...] = jnp.broadcast_to(rows[None], p1.shape)


def backward(nbd, R, C, origins, slots, g1, w_ref, wr, part, cb):
    me_r = lax.axis_index("row")
    me_c = lax.axis_index("col")
    bsz = slots[0].shape[1]
    rb = w_ref.shape[0] // R
    rio = iota((rb, bsz), 0).astype(F32)
    cio = iota((cb, bsz), 0).astype(F32)
    for s, slot in enumerate(slots):
        q = origins(me_r, s)
        w = w_ref[pl.ds(pl.multiple_of(q * rb, rb), rb), :]
        tile = g1[q * C + me_c]
        for k in range(nbd):
            pick = jnp.where(rio == tile[nbd + k : nbd + k + 1, :], w, 0.0)
            wr[s * nbd + k : s * nbd + k + 1, :] = jnp.sum(pick, axis=0, keepdims=True)
    wt = wr[...].T
    for s, slot in enumerate(slots):
        q = origins(me_r, s)
        cols = slot[slot.shape[0] - up(nbd, 8) :, :]
        total = jnp.zeros((cb, bsz), F32)
        for k in range(nbd):
            i = s * nbd + k
            prod = jnp.sum(
                slot[k * bsz : (k + 1) * bsz, :] * wt[:, i : i + 1], axis=0, keepdims=True
            )
            total += jnp.where(cio == cols[k : k + 1, :], prod, 0.0)
        part[q] = total
    out = part[0]
    for q in range(1, R):
        out += part[q]
    return out


def primal_kernel(nbd, R, C, origins, g1, *refs):
    slots = refs[:R]
    x_prev, cost, upper, steps, x_new, dr, dc, p3, w_ref, wr, part = refs[R:]
    me_r = lax.axis_index("row")
    me_c = lax.axis_index("col")
    bsz = x_prev.shape[1]
    cb = x_prev.shape[0]
    rb = dr.shape[0] // R
    base = nbd * bsz
    rio = iota((rb, bsz), 0).astype(F32)
    cio = iota((cb, bsz), 0).astype(F32)
    wr[...] = jnp.zeros_like(wr)
    for q in range(R):

        def body(c, acc):
            tile = g1[q * C + c]
            for k in range(nbd):
                hit = rio == tile[nbd + k : nbd + k + 1, :]
                acc = jnp.maximum(acc, jnp.where(hit, tile[k : k + 1, :], 0.0))
            return acc

        peak = lax.fori_loop(0, C, body, jnp.zeros((rb, bsz), F32), unroll=min(C, 8))
        dr[q * rb : (q + 1) * rb, :] = 1.0 / jnp.sqrt(jnp.maximum(peak, 0.5))
    colmax = jnp.zeros((cb, bsz), F32)
    for s, slot in enumerate(slots):
        q = origins(me_r, s)
        tile = g1[q * C + me_c]
        cols = slot[slot.shape[0] - up(nbd, 8) :, :]
        at = pl.ds(pl.multiple_of(q * rb, rb), rb)
        w_ref[at, :] = dr[at, :] * slot[base : base + rb, :]
        for k in range(nbd):
            a = slot[k * bsz : (k + 1) * bsz, :]
            cp = jnp.max(jnp.abs(a), axis=0, keepdims=True)
            hit = (cio == cols[k : k + 1, :]) & (tile[nbd + k : nbd + k + 1, :] >= 0.0)
            colmax = jnp.maximum(colmax, jnp.where(hit, cp, 0.0))
    scale = 1.0 / jnp.sqrt(jnp.maximum(colmax, 0.5))
    dc[...] = scale
    got = backward(nbd, R, C, origins, slots, g1, w_ref, wr, part, cb)
    tau = steps[0] / steps[1]
    grad = scale * cost[...] - got * scale
    xp = x_prev[...]
    xn = jnp.clip(xp - tau * grad, 0.0, upper[...] / scale)
    x_new[...] = xn
    v1 = scale * xn
    v2 = scale * (xn - xp)
    own = slots[0]
    cols = own[own.shape[0] - up(nbd, 8) :, :]
    res = []
    for k in range(nbd):
        a = own[k * bsz : (k + 1) * bsz, :]
        hit = cio == cols[k : k + 1, :]
        for v in (v1, v2):
            vk = jnp.sum(jnp.where(hit, v, 0.0), axis=0, keepdims=True)
            res.append(jnp.sum(a * vk, axis=1, keepdims=True))
    rows = rows_of(res, bsz)[: p3.shape[1]]
    p3[...] = jnp.broadcast_to(rows[None], p3.shape)


def dual_kernel(nbd, R, C, origins, g1, g3, *refs):
    slots = refs[:R]
    x_prev, cost, upper, steps, x_new, dr, dc, y_new, p4, dual, w_ref, wr, part = refs[R:]
    me_r = lax.axis_index("row")
    bsz = x_prev.shape[1]
    cb = x_prev.shape[0]
    rb = dr.shape[0] // R
    base = nbd * bsz
    rio = iota((rb, bsz), 0).astype(F32)
    wr[...] = jnp.zeros_like(wr)
    sigma = steps[0] * steps[1]
    dr_all = []
    for s, slot in enumerate(slots):
        q = origins(me_r, s)
        at = pl.ds(pl.multiple_of(q * rb, rb), rb)

        def body(c, acc):
            one, two = acc
            tile = g1[q * C + c]
            got = g3[q * C + c]
            for k in range(nbd):
                hit = rio == tile[nbd + k : nbd + k + 1, :]
                one = one + jnp.where(hit, got[2 * k : 2 * k + 1, :], 0.0)
                two = two + jnp.where(hit, got[2 * k + 1 : 2 * k + 2, :], 0.0)
            return one, two

        zero = jnp.zeros((rb, bsz), F32)
        ax, adx = lax.fori_loop(0, C, body, (zero, zero), unroll=min(C, 8))
        scale = dr[at, :]
        ax = ax * scale
        adx = adx * scale
        bs = scale * slot[base + rb : base + 2 * rb, :]
        yp = slot[base : base + rb, :]
        yn = yp + sigma * (bs - ax - adx)
        if s == 0:
            y_new[...] = yn
        w_ref[at, :] = scale * yn
        dy = yn - yp
        resid = bs - ax
        for i, term in enumerate((dy * dy, adx * adx, resid * resid, bs * yn)):
            part[q, i : i + 1, :] = jnp.sum(term, axis=0, keepdims=True)
    sums = part[0, :4, :]
    for q in range(1, R):
        sums += part[q, :4, :]
    dual[...] = jnp.broadcast_to(jnp.sum(sums, axis=1, keepdims=True), dual.shape)
    got = backward(nbd, R, C, origins, slots, g1, w_ref, wr, part, cb)
    scale = dc[...]
    cs = scale * cost[...]
    reduced = cs - got * scale
    us = upper[...] / scale
    xn = x_new[...]
    dx = xn - x_prev[...]
    lane = iota((1, bsz), 1)
    out = jnp.zeros((1, bsz), F32)
    for i, term in enumerate((dx * dx, cs * xn, us * jnp.maximum(-reduced, 0.0))):
        out = jnp.where(lane == i, jnp.sum(term), out)
    p4[...] = jnp.broadcast_to(out, p4.shape)


def stats_kernel(total_rows, total_cols, g4, dual, steps, stats):
    bsz = g4.shape[1]
    primal = jnp.sum(g4[...], axis=0, keepdims=True)
    lane = iota((1, bsz), 1)

    def pick(i):
        return jnp.sum(jnp.where(lane == i, primal, 0.0), axis=1, keepdims=True)

    dx2, cx, uneg = (jnp.broadcast_to(pick(i), (1, bsz)) for i in range(3))
    dy2, adx2, res2, by = (dual[i : i + 1, :] for i in range(4))
    omega = steps[1]
    movement = 0.5 * omega * dx2 + 0.5 / omega * dy2
    first = jnp.sqrt(res2 / total_rows)
    second = (cx - by + uneg) / total_cols
    third = movement / jnp.sqrt(adx2 * dy2 + 1e-06)
    out = jnp.where(lane == 0, first, jnp.where(lane == 1, second, third))
    stats[...] = out[:, : stats.shape[1]]


def shards(blocks, block_rows, block_cols, counts, x_prev, y_prev, cost, rhs, upper, steps):
    R = lax.axis_size("row")
    C = lax.axis_size("col")
    ndev = R * C
    nbd, bsz = blocks.shape[2], blocks.shape[3]
    rb = y_prev.shape[0] // bsz
    cb = x_prev.shape[0] // bsz
    hp = up(2 * nbd, 8)
    flat = blocks.reshape(nbd * bsz, bsz)
    y2, rhs2 = y_prev.reshape(rb, bsz), rhs.reshape(rb, bsz)
    x2, cost2, upper2 = (v.reshape(cb, bsz) for v in (x_prev, cost, upper))
    params = pltpu.CompilerParams(vmem_limit_bytes=LIMIT)
    bulk_rows = nbd * bsz + 2 * rb + up(nbd, 8)
    p1, bulk = pl.pallas_call(
        functools.partial(peaks_kernel, nbd),
        out_shape=(
            jax.ShapeDtypeStruct((ndev, hp, bsz), F32),
            jax.ShapeDtypeStruct((bulk_rows, bsz), F32),
        ),
        in_specs=[VMEM] * 3 + [SMEM] * 3,
        out_specs=(VMEM, VMEM),
        compiler_params=params,
        name="peaks",
    )(flat, y2, rhs2, block_rows.reshape(nbd), block_cols.reshape(nbd), counts.reshape(1))

    def spread(v):
        return lax.all_to_all(v, ("row", "col"), 0, 0, tiled=True)

    slots, ids = [bulk], [0]
    if R & (R - 1) == 0:
        step = R // 2
        while step:
            perm = [(i, i ^ step) for i in range(R)]
            slots += [lax.ppermute(b, "row", perm) for b in slots]
            ids += [i ^ step for i in ids]
            step //= 2

        def origins(me, s):
            return me ^ ids[s] if ids[s] else me

    else:
        for step in range(1, R):
            slots.append(lax.ppermute(bulk, "row", [(i, (i - step) % R) for i in range(R)]))

        def origins(me, s):
            return lax.rem(me + s, R)

    g1 = spread(p1)
    scratch = [
        pltpu.VMEM((R * rb, bsz), F32),
        pltpu.VMEM((up(R * nbd, bsz), bsz), F32),
        pltpu.VMEM((R, cb, bsz), F32),
    ]
    x_new, dr, dc, p3 = pl.pallas_call(
        functools.partial(primal_kernel, nbd, R, C, origins),
        out_shape=(
            jax.ShapeDtypeStruct((cb, bsz), F32),
            jax.ShapeDtypeStruct((R * rb, bsz), F32),
            jax.ShapeDtypeStruct((cb, bsz), F32),
            jax.ShapeDtypeStruct((ndev, hp, bsz), F32),
        ),
        in_specs=[VMEM] * (1 + R + 3) + [SMEM],
        out_specs=(VMEM,) * 4,
        scratch_shapes=scratch,
        compiler_params=params,
        name="primal",
    )(g1, *slots, x2, cost2, upper2, steps)
    g3 = spread(p3)
    y_new, p4, dual = pl.pallas_call(
        functools.partial(dual_kernel, nbd, R, C, origins),
        out_shape=(
            jax.ShapeDtypeStruct((rb, bsz), F32),
            jax.ShapeDtypeStruct((C, bsz), F32),
            jax.ShapeDtypeStruct((4, bsz), F32),
        ),
        in_specs=[VMEM] * (2 + R + 3) + [SMEM] + [VMEM] * 3,
        out_specs=(VMEM,) * 3,
        scratch_shapes=scratch,
        compiler_params=params,
        name="dual",
    )(g1, g3, *slots, x2, cost2, upper2, steps, x_new, dr, dc)
    g4 = lax.all_to_all(p4, "col", 0, 0, tiled=True)
    stats = pl.pallas_call(
        functools.partial(
            stats_kernel, float(y_prev.shape[0] * R), float(x_prev.shape[0] * C)
        ),
        out_shape=jax.ShapeDtypeStruct((1, 3), F32),
        in_specs=[VMEM, VMEM, SMEM],
        out_specs=VMEM,
        compiler_params=params,
        name="stats",
    )(g4, dual, steps)
    return (x_new.reshape(-1), y_new.reshape(-1), stats.reshape(-1))


def solution(mesh):
    placed = (
        P("row", "col", None, None, None),
        P("row", "col", None),
        P("row", "col", None),
        P("row", "col"),
        P("col"),
        P("row"),
        P("col"),
        P("row"),
        P("col"),
        P(),
    )
    return jax.shard_map(
        shards, mesh=mesh, in_specs=placed, out_specs=(P("col"), P("row"), P()), check_vma=False
    )
```

time: 156 us -> 55.7 us (0.36)
  blocking collectives: 127 us -> 33.3 us
  between operations: 10.4 us -> 1.34 us
  waiting for transfers between devices: 0 us -> 7.1 us
  other arithmetic: 6.2 us -> 0 us
  Pallas kernels: 0 us -> 6.1 us
  local copies, waits for them, and re-layouts: 7.97 us -> 4.39 us
  starting transfers between devices: 0 us -> 3.01 us
  matrix products: 2.7 us -> 0 us
    psum x4 -> x0, blocking collectives: 81.5 us -> none  [the longest x1 36.8 us: shards(): lax.psum(jnp.concatenate([primal_terms, dual_terms]), ('row', 'col'))]
    pmax x2 -> x0, blocking collectives: 45.7 us -> none  [the longest x1 37.4 us: shards(): rowmax = lax.pmax(rpeak, 'col')]
    all_to_all x0 -> x3, blocking collectives: none -> 33.3 us  [the longest x2 23.7 us: spread(): return lax.all_to_all(v, ('row', 'col'), 0, 0, tiled=True)]
    ppermute x0 -> x3, waiting for transfers between devices: none -> 7.1 us  [shards(): slots += [lax.ppermute(b, 'row', perm) for b in slots]]
    pallas_call x0 -> x4, Pallas kernels: none -> 6.1 us  [the longest x1 2.14 us: shards(): pl.pallas_call(functools.partial(dual_kernel, nbd, R, C, origins), out_sh...]
    concatenate x1 -> x0, local copies, waits for them, and re-layouts: 4.46 us -> none  [shards(): jnp.concatenate([primal_terms, dual_terms])]
    ppermute x0 -> x3, starting transfers between devices: none -> 3.01 us  [shards(): slots += [lax.ppermute(b, 'row', perm) for b in slots]]
    unnamed x21 -> x20, local copies, waits for them, and re-layouts: 1.42 us -> 4.39 us
  transfers between devices with their start and end apart: 0 -> 3, of which waited for: 0 -> 1; matrix products, arithmetic and copies ran while one was open for 0% -> 0% of each run, Pallas kernels for 0% -> 0%
where the time goes in v1:
time: 55.7 us; the launch traced here: 55.2 us
  blocking collectives  33.3 us (60%)
  waiting for transfers between devices  7.1 us (13%)
  Pallas kernels  6.1 us (11%)
  local copies, waits for them, and re-layouts  4.39 us (8%)
  starting transfers between devices  3.01 us (5%)
  between operations  1.34 us (2%)
    all_to_all x2, blocking collectives, spread(): return lax.all_to_all(v, ('row', 'col'), 0, 0, tiled=True)  23.7 us
    all_to_all x1, blocking collectives, shards(): g4 = lax.all_to_all(p4, 'col', 0, 0, tiled=True)  9.57 us
    ppermute x3, waiting for transfers between devices, shards(): slots += [lax.ppermute(b, 'row', perm) for b in slots]  7.1 us
    unnamed x20, local copies, waits for them, and re-layouts  4.39 us
    ppermute x3, starting transfers between devices, shards(): slots += [lax.ppermute(b, 'row', perm) for b in slots]  3.01 us
    pallas_call x1, Pallas kernels, shards(): pl.pallas_call(functools.partial(dual_kernel, nbd, R, C, origins), out_sh...  2.14 us
    pallas_call x1, Pallas kernels, shards(): pl.pallas_call(functools.partial(primal_kernel, nbd, R, C, origins), out_...  2.09 us
    pallas_call x1, Pallas kernels, shards(): pl.pallas_call(functools.partial(stats_kernel, float(y_prev.shape[0] * R)...  1.14 us
  transfers between devices with their start and end apart: 3, of which 1 were waited for; matrix products, arithmetic and copies ran while one was open for 0% of the time, Pallas kernels for 0%

profile of v1, /device:TPU:0, one launch (start us, length us, event | category | flops | bytes accessed | tf_op | source)
XLA Modules:
  0.0 55.2 jit_solution(12987552894292561500)
XLA Ops:
  1.3 0.0 copy-start.8
  1.3 0.0 copy-start.9
  1.3 0.6 %copy-done.8 = s32[1,1,4]{2,1,0:T(1,128)S(1)} copy-done((s32[1,1,4]{2,1,0:T(1,128)S(1)}, s32[1,1,4]{2,1,0:T(1,128)}, u32[]{:S(2)}) %copy-start.8) | copy-done | bytes 40
  1.9 0.0 copy-done.9
  1.9 0.0 copy-start
  2.0 0.9 %copy-done = f32[1,1,4,128,128]{4,3,2,1,0:T(8,128)S(1)} copy-done((f32[1,1,4,128,128]{4,3,2,1,0:T(8,128)S(1)}, f32[1,1,4,128,128]{4,3,2,1,0:T(8,128)}, u32[]{:S(2)}) %copy-start) | copy-done | bytes 262168
  2.9 0.0 copy-start.4
  2.9 0.7 %copy-done.4 = f32[4096]{0:T(1024)S(1)} copy-done((f32[4096]{0:T(1024)S(1)}, f32[4096]{0:T(1024)}, u32[]{:S(2)}) %copy-start.4) | copy-done | bytes 16408
  3.6 0.0 copy-start.5
  3.6 0.7 %copy-done.5 = f32[4096]{0:T(1024)S(1)} copy-done((f32[4096]{0:T(1024)S(1)}, f32[4096]{0:T(1024)}, u32[]{:S(2)}) %copy-start.5) | copy-done | bytes 16408
  4.3 0.7 %peaks.1 = (f32[32,8,128]{2,1,0:T(8,128)S(1)}, f32[584,128]{1,0:T(8,128)S(1)}) custom-call(f32[512,128]{1,0:T(8,128)S(1)} %bitcast.17, f32[32,128]{1,0:T(8,128)S(1)} %bitcast.24, f32[32,128]{1,0:T(8,128)S(1)} %bitcast.25, s32[4]{0:T(128)S(1)} %bitcast.29, s32[4]{0:T(128)S(1)} %bitcast.30, s32[1]{0:T(128)} %bitcast.16.count), custom_call_target="tpu_custom_call" | custom-call | tf_op jit(solution)/shard_map/peaks/pallas_call | solution.py:238
  5.1 3.0 %collective-permute-start = (f32[584,128]{1,0:T(8,128)S(1)}, f32[584,128]{1,0:T(8,128)S(1)}, u32[]{:S(2)}, u32[]{:S(2)}) collective-permute-start(f32[584,128]{1,0:T(8,128)S(1)} %get-tuple-element.13.refs_0_), channel_id=1, source_target_pairs={{0,16},{8,24},{16,0},{24,8},{1,17},{9,25},{17,1},{25,9},{2,18},{10... | collective-permute-start | bytes 897032 | tf_op jit(solution)/shard_map/ppermute | solution.py:258
  8.1 0.0 collective-permute-start.1
  8.1 7.1 %collective-permute-done.refs_1_ = f32[584,128]{1,0:T(8,128)S(1)} collective-permute-done((f32[584,128]{1,0:T(8,128)S(1)}, f32[584,128]{1,0:T(8,128)S(1)}, u32[]{:S(2)}, u32[]{:S(2)}) %collective-permute-start) | collective-permute-done | bytes 299040 | tf_op jit(solution)/shard_map/ppermute | solution.py:258
  15.2 0.0 collective-permute-start.2
  15.2 0.0 copy-start.2
  15.2 0.0 copy-start.3
  15.2 13.7 %all_to_all.21.g1 = f32[32,8,128]{2,1,0:T(8,128)S(1)} all-to-all(f32[32,8,128]{2,1,0:T(8,128)S(1)} %get-tuple-element.12), channel_id=1, replica_groups=mesh['row'=4,'col'=8] {'row','col'}, dimensions={0} | all-to-all | bytes 262144 | tf_op jit(solution)/shard_map/all_to_all | solution.py:251
  28.9 0.0 copy-start.1
  28.9 0.0 collective-permute-done.1.refs_2_
  28.9 0.0 collective-permute-done.2.refs_3_
  28.9 0.0 copy-start.6
  28.9 0.0 copy-done.2
  29.0 0.0 copy-done.3
  29.0 0.6 %copy-done.1 = f32[1024]{0:T(1024)S(1)} copy-done((f32[1024]{0:T(1024)S(1)}, f32[1024]{0:T(1024)}, u32[]{:S(2)}) %copy-start.1) | copy-done | bytes 4120
  29.6 0.0 copy-done.6
  29.6 2.1 %primal.1 = (f32[8,128]{1,0:T(8,128)}, f32[128,128]{1,0:T(8,128)S(1)}, f32[8,128]{1,0:T(8,128)S(1)}, f32[32,8,128]{2,1,0:T(8,128)S(1)}) custom-call(f32[32,8,128]{2,1,0:T(8,128)S(1)} %all_to_all.21.g1, f32[584,128]{1,0:T(8,128)S(1)} %get-tuple-element.13.refs_0_, f32[584,128]{1,0:T(8,128)S(1)} %collective-permute-done.refs_1_, ...), custom_call_target="tpu_custom_call" | custom-call | tf_op jit(solution)/shard_map/primal/pallas_call | solution.py:278
  31.7 10.0 %all_to_all.22.g3 = f32[32,8,128]{2,1,0:T(8,128)S(1)} all-to-all(f32[32,8,128]{2,1,0:T(8,128)S(1)} %get-tuple-element.15), channel_id=1, replica_groups=mesh['row'=4,'col'=8] {'row','col'}, dimensions={0} | all-to-all | bytes 262144 | tf_op jit(solution)/shard_map/all_to_all | solution.py:251
  41.7 0.0 copy-start.7
  41.7 0.7 %copy-done.7 = f32[8,128]{1,0:T(8,128)S(1)} copy-done((f32[8,128]{1,0:T(8,128)S(1)}, f32[8,128]{1,0:T(8,128)}, u32[]{:S(2)}) %copy-start.7) | copy-done | bytes 4120
  42.4 2.1 %dual.1 = (f32[32,128]{1,0:T(8,128)}, f32[8,128]{1,0:T(8,128)S(1)}, f32[4,128]{1,0:T(4,128)S(1)}) custom-call(f32[32,8,128]{2,1,0:T(8,128)S(1)} %all_to_all.21.g1, f32[32,8,128]{2,1,0:T(8,128)S(1)} %all_to_all.22.g3, f32[584,128]{1,0:T(8,128)S(1)} %get-tuple-element.13.refs_0_, f32[584,128]{1,0:T(8,128)S(1)} %collective-permute-done.refs_1_, ...), custom_call_target="tpu_custom_call" | custom-call | tf_op jit(solution)/shard_map/dual/pallas_call | solution.py:293
  44.5 9.6 %all_to_all.23 = f32[8,1,128]{2,1,0:T(1,128)S(1)} all-to-all(f32[8,1,128]{2,1,0:T(1,128)S(1)} %bitcast.28), channel_id=1, replica_groups=mesh['row'=4,'col'=8] {'col'}, dimensions={0} | all-to-all | bytes 8192 | tf_op jit(solution)/shard_map/all_to_all | solution.py:306
  54.1 1.1 %stats.1 = f32[1,3]{1,0:T(1,128)} custom-call(f32[8,128]{1,0:T(8,128)S(1)} %bitcast.26, f32[4,128]{1,0:T(4,128)S(1)} %get-tuple-element.20.dual, f32[2]{0:T(128)S(1)} %copy-done.6), custom_call_target="tpu_custom_call" | custom-call | tf_op jit(solution)/shard_map/stats/pallas_call | solution.py:307
Async XLA Ops:
  1.3 0.7 %copy-start.8 = (s32[1,1,4]{2,1,0:T(1,128)S(1)}, s32[1,1,4]{2,1,0:T(1,128)}, u32[]{:S(2)}) copy-start(s32[1,1,4]{2,1,0:T(1,128)} %param.11) | copy-start | bytes 52
  1.3 0.7 %copy-start.9 = (s32[1,1,4]{2,1,0:T(1,128)S(1)}, s32[1,1,4]{2,1,0:T(1,128)}, u32[]{:S(2)}) copy-start(s32[1,1,4]{2,1,0:T(1,128)} %param.12) | copy-start | bytes 52
  1.9 0.9 %copy-start = (f32[1,1,4,128,128]{4,3,2,1,0:T(8,128)S(1)}, f32[1,1,4,128,128]{4,3,2,1,0:T(8,128)}, u32[]{:S(2)}) copy-start(f32[1,1,4,128,128]{4,3,2,1,0:T(8,128)} %param.10) | copy-start | bytes 786436
  2.9 0.7 %copy-start.4 = (f32[4096]{0:T(1024)S(1)}, f32[4096]{0:T(1024)}, u32[]{:S(2)}) copy-start(f32[4096]{0:T(1024)} %param.15) | copy-start | bytes 49156
  3.6 0.7 %copy-start.5 = (f32[4096]{0:T(1024)S(1)}, f32[4096]{0:T(1024)}, u32[]{:S(2)}) copy-start(f32[4096]{0:T(1024)} %param.17) | copy-start | bytes 49156
  5.1 10.1 %collective-permute-start = (f32[584,128]{1,0:T(8,128)S(1)}, f32[584,128]{1,0:T(8,128)S(1)}, u32[]{:S(2)}, u32[]{:S(2)}) collective-permute-start(f32[584,128]{1,0:T(8,128)S(1)} %get-tuple-element.13.refs_0_), channel_id=1, source_target_pairs={{0,16},{8,24},{16,0},{24,8},{1,17},{9,25},{17,1},{25,9},{2,18},{10... | collective-permute-start | bytes 897032 | tf_op jit(solution)/shard_map/ppermute | solution.py:258
  8.1 20.9 %collective-permute-start.1 = (f32[584,128]{1,0:T(8,128)S(1)}, f32[584,128]{1,0:T(8,128)S(1)}, u32[]{:S(2)}, u32[]{:S(2)}) collective-permute-start(f32[584,128]{1,0:T(8,128)S(1)} %get-tuple-element.13.refs_0_), channel_id=1, source_target_pairs={{0,8},{8,0},{16,24},{24,16},{1,9},{9,1},{17,25},{25,17},{2,10},{10... | collective-permute-start | bytes 897032 | tf_op jit(solution)/shard_map/ppermute | solution.py:258
  15.2 13.8 %collective-permute-start.2 = (f32[584,128]{1,0:T(8,128)S(1)}, f32[584,128]{1,0:T(8,128)S(1)}, u32[]{:S(2)}, u32[]{:S(2)}) collective-permute-start(f32[584,128]{1,0:T(8,128)S(1)} %collective-permute-done.refs_1_), channel_id=1, source_target_pairs={{0,8},{8,0},{16,24},{24,16},{1,9},{9,1},{17,25},{25,17},{2,10},{10... | collective-permute-start | bytes 897032 | tf_op jit(solution)/shard_map/ppermute | solution.py:258
  15.2 13.8 %copy-start.2 = (f32[1024]{0:T(1024)S(1)}, f32[1024]{0:T(1024)}, u32[]{:S(2)}) copy-start(f32[1024]{0:T(1024)} %param.16) | copy-start | bytes 12292
  15.2 13.8 %copy-start.3 = (f32[1024]{0:T(1024)S(1)}, f32[1024]{0:T(1024)}, u32[]{:S(2)}) copy-start(f32[1024]{0:T(1024)} %param.18) | copy-start | bytes 12292
  28.9 0.7 %copy-start.1 = (f32[1024]{0:T(1024)S(1)}, f32[1024]{0:T(1024)}, u32[]{:S(2)}) copy-start(f32[1024]{0:T(1024)} %param.14) | copy-start | bytes 12292
  28.9 0.7 %copy-start.6 = (f32[2]{0:T(128)S(1)}, f32[2]{0:T(128)}, u32[]{:S(2)}) copy-start(f32[2]{0:T(128)} %steps.1) | copy-start | bytes 28
  41.7 0.7 %copy-start.7 = (f32[8,128]{1,0:T(8,128)S(1)}, f32[8,128]{1,0:T(8,128)}, u32[]{:S(2)}) copy-start(f32[8,128]{1,0:T(8,128)} %get-tuple-element.14.refs_8_) | copy-start | bytes 12292

commit v2 on v1

--- a/solution.py
+++ b/solution.py
@@ -10,6 +10,7 @@
 F32 = jnp.float32
 VMEM = pl.BlockSpec(memory_space=pltpu.VMEM)
 SMEM = pl.BlockSpec(memory_space=pltpu.SMEM)
+HBM = pl.BlockSpec(memory_space=pltpu.HBM)
 LIMIT = 40 * 1024 * 1024
 
 
@@ -29,28 +30,49 @@
     return cols.T
 
 
-def peaks_kernel(nbd, blocks, y, rhs, brow, bcol, count, p1, bulk):
-    bsz = blocks.shape[1]
+def peaks_kernel(nbd, blocks, y, rhs, x, cost, upper, brow, bcol, steps, count, p1, bulk, aux, *scratch):
+    s_row, s_col, s_steps, sems = scratch
+    bsz = bulk.shape[1]
     hp = p1.shape[1]
     rb = y.shape[0]
+    cb = x.shape[0]
+    base = nbd * bsz
+    pairs = [
+        (brow, s_row),
+        (bcol, s_col),
+        (steps, s_steps),
+        (y, bulk.at[base : base + rb]),
+        (rhs, bulk.at[base + rb : base + 2 * rb]),
+        (x, aux.at[:cb]),
+        (cost, aux.at[cb : 2 * cb]),
+        (upper, aux.at[2 * cb : 3 * cb]),
+    ]
+    loads = [
+        pltpu.make_async_copy(blocks.at[k], bulk.at[k * bsz : (k + 1) * bsz], sems.at[k])
+        for k in range(nbd)
+    ]
+    rest = [pltpu.make_async_copy(a, b, sems.at[nbd + i]) for i, (a, b) in enumerate(pairs)]
+    for copy in loads + rest:
+        copy.start()
     peaks = []
     for k in range(nbd):
-        a = blocks[k * bsz : (k + 1) * bsz, :]
-        bulk[k * bsz : (k + 1) * bsz, :] = a
+        loads[k].wait()
+        a = bulk[k * bsz : (k + 1) * bsz, :]
         peaks.append(jnp.max(jnp.abs(a), axis=1, keepdims=True))
     rows = rows_of(peaks, bsz)[:hp]
+    for copy in rest:
+        copy.wait()
     sub = iota((hp, bsz), 0)
-    base = nbd * bsz
-    bulk[base : base + rb, :] = y[...]
-    bulk[base + rb : base + 2 * rb, :] = rhs[...]
     ch = bulk.shape[0] - base - 2 * rb
     csub = iota((ch, bsz), 0)
     cols = jnp.zeros((ch, bsz), F32)
     for k in range(nbd):
-        code = jnp.where(k < count[0], brow[k], -1).astype(F32)
+        code = jnp.where(k < count[0, 0], s_row[0, 0, k], -1).astype(F32)
         rows = jnp.where(sub == nbd + k, code, rows)
-        cols = jnp.where(csub == k, bcol[k].astype(F32), cols)
+        cols = jnp.where(csub == k, s_col[0, 0, k].astype(F32), cols)
     bulk[base + 2 * rb :, :] = cols
+    asub = iota((8, bsz), 0)
+    aux[3 * cb :, :] = jnp.where(asub == 0, s_steps[0], s_steps[1])
     p1[...] = jnp.broadcast_to(rows[None], p1.shape)
 
 
@@ -88,11 +110,12 @@
 
 def primal_kernel(nbd, R, C, origins, g1, *refs):
     slots = refs[:R]
-    x_prev, cost, upper, steps, x_new, dr, dc, p3, w_ref, wr, part = refs[R:]
+    aux, x_new, dr, dc, p3, w_ref, wr, part = refs[R:]
     me_r = lax.axis_index("row")
     me_c = lax.axis_index("col")
-    bsz = x_prev.shape[1]
-    cb = x_prev.shape[0]
+    cb, bsz = x_new.shape
+    x_prev, cost, upper = (aux.at[i * cb : (i + 1) * cb] for i in range(3))
+    eta, omega = (aux[3 * cb + i : 3 * cb + i + 1, :] for i in range(2))
     rb = dr.shape[0] // R
     base = nbd * bsz
     rio = iota((rb, bsz), 0).astype(F32)
@@ -124,7 +147,7 @@
     scale = 1.0 / jnp.sqrt(jnp.maximum(colmax, 0.5))
     dc[...] = scale
     got = backward(nbd, R, C, origins, slots, g1, w_ref, wr, part, cb)
-    tau = steps[0] / steps[1]
+    tau = eta / omega
     grad = scale * cost[...] - got * scale
     xp = x_prev[...]
     xn = jnp.clip(xp - tau * grad, 0.0, upper[...] / scale)
@@ -146,15 +169,16 @@
 
 def dual_kernel(nbd, R, C, origins, g1, g3, *refs):
     slots = refs[:R]
-    x_prev, cost, upper, steps, x_new, dr, dc, y_new, p4, dual, w_ref, wr, part = refs[R:]
+    aux, x_new, dr, dc, y_new, p4, dual, w_ref, wr, part = refs[R:]
     me_r = lax.axis_index("row")
-    bsz = x_prev.shape[1]
-    cb = x_prev.shape[0]
+    cb, bsz = x_new.shape
+    x_prev, cost, upper = (aux.at[i * cb : (i + 1) * cb] for i in range(3))
+    eta, omega = (aux[3 * cb + i : 3 * cb + i + 1, :] for i in range(2))
     rb = dr.shape[0] // R
     base = nbd * bsz
     rio = iota((rb, bsz), 0).astype(F32)
     wr[...] = jnp.zeros_like(wr)
-    sigma = steps[0] * steps[1]
+    sigma = eta * omega
     dr_all = []
     for s, slot in enumerate(slots):
         q = origins(me_r, s)
@@ -188,7 +212,8 @@
     sums = part[0, :4, :]
     for q in range(1, R):
         sums += part[q, :4, :]
-    dual[...] = jnp.broadcast_to(jnp.sum(sums, axis=1, keepdims=True), dual.shape)
+    dual[:4, :] = jnp.broadcast_to(jnp.sum(sums, axis=1, keepdims=True), (4, bsz))
+    dual[4:, :] = jnp.broadcast_to(omega, (4, bsz))
     got = backward(nbd, R, C, origins, slots, g1, w_ref, wr, part, cb)
     scale = dc[...]
     cs = scale * cost[...]
@@ -203,7 +228,13 @@
     p4[...] = jnp.broadcast_to(out, p4.shape)
 
 
-def stats_kernel(total_rows, total_cols, g4, dual, steps, stats):
+def stats_kernel(total_rows, total_cols, g4, dual, x_new, y_new, stats, x_out, y_out, sems):
+    outs = [
+        pltpu.make_async_copy(x_new, x_out, sems.at[0]),
+        pltpu.make_async_copy(y_new, y_out, sems.at[1]),
+    ]
+    for copy in outs:
+        copy.start()
     bsz = g4.shape[1]
     primal = jnp.sum(g4[...], axis=0, keepdims=True)
     lane = iota((1, bsz), 1)
@@ -213,13 +244,15 @@
 
     dx2, cx, uneg = (jnp.broadcast_to(pick(i), (1, bsz)) for i in range(3))
     dy2, adx2, res2, by = (dual[i : i + 1, :] for i in range(4))
-    omega = steps[1]
+    omega = dual[4:5, :]
     movement = 0.5 * omega * dx2 + 0.5 / omega * dy2
     first = jnp.sqrt(res2 / total_rows)
     second = (cx - by + uneg) / total_cols
     third = movement / jnp.sqrt(adx2 * dy2 + 1e-06)
     out = jnp.where(lane == 0, first, jnp.where(lane == 1, second, third))
     stats[...] = out[:, : stats.shape[1]]
+    for copy in outs:
+        copy.wait()
 
 
 def shards(blocks, block_rows, block_cols, counts, x_prev, y_prev, cost, rhs, upper, steps):
@@ -230,46 +263,53 @@
     rb = y_prev.shape[0] // bsz
     cb = x_prev.shape[0] // bsz
     hp = up(2 * nbd, 8)
-    flat = blocks.reshape(nbd * bsz, bsz)
     y2, rhs2 = y_prev.reshape(rb, bsz), rhs.reshape(rb, bsz)
     x2, cost2, upper2 = (v.reshape(cb, bsz) for v in (x_prev, cost, upper))
     params = pltpu.CompilerParams(vmem_limit_bytes=LIMIT)
     bulk_rows = nbd * bsz + 2 * rb + up(nbd, 8)
-    p1, bulk = pl.pallas_call(
+    p1, bulk, aux = pl.pallas_call(
         functools.partial(peaks_kernel, nbd),
         out_shape=(
             jax.ShapeDtypeStruct((ndev, hp, bsz), F32),
             jax.ShapeDtypeStruct((bulk_rows, bsz), F32),
-        ),
-        in_specs=[VMEM] * 3 + [SMEM] * 3,
-        out_specs=(VMEM, VMEM),
+            jax.ShapeDtypeStruct((3 * cb + 8, bsz), F32),
+        ),
+        in_specs=[HBM] * 9 + [SMEM],
+        out_specs=(VMEM,) * 3,
+        scratch_shapes=[
+            pltpu.SMEM((1, 1, nbd), jnp.int32),
+            pltpu.SMEM((1, 1, nbd), jnp.int32),
+            pltpu.SMEM(steps.shape, F32),
+            pltpu.SemaphoreType.DMA((nbd + 8,)),
+        ],
         compiler_params=params,
         name="peaks",
-    )(flat, y2, rhs2, block_rows.reshape(nbd), block_cols.reshape(nbd), counts.reshape(1))
+    )(
+        *(
+            pltpu.with_memory_space_constraint(v, pltpu.HBM)
+            for v in (blocks[0, 0], y2, rhs2, x2, cost2, upper2, block_rows, block_cols, steps)
+        ),
+        counts,
+    )
 
     def spread(v):
         return lax.all_to_all(v, ("row", "col"), 0, 0, tiled=True)
 
-    slots, ids = [bulk], [0]
-    if R & (R - 1) == 0:
-        step = R // 2
-        while step:
-            perm = [(i, i ^ step) for i in range(R)]
-            slots += [lax.ppermute(b, "row", perm) for b in slots]
-            ids += [i ^ step for i in ids]
-            step //= 2
-
-        def origins(me, s):
-            return me ^ ids[s] if ids[s] else me
-
-    else:
-        for step in range(1, R):
-            slots.append(lax.ppermute(bulk, "row", [(i, (i - step) % R) for i in range(R)]))
-
-        def origins(me, s):
-            return lax.rem(me + s, R)
-
-    g1 = spread(p1)
+    step = R // 2
+    ids, slots = [0], [bulk]
+    g1 = None
+    while step:
+        perm = [(i, i ^ step) for i in range(R)]
+        slots += [lax.ppermute(b, "row", perm) for b in slots]
+        ids += [i ^ step for i in ids]
+        if g1 is None:
+            g1 = spread(p1)
+            g1, *slots[1:] = lax.optimization_barrier((g1, *slots[1:]))
+        step //= 2
+
+    def origins(me, s):
+        return me ^ ids[s] if ids[s] else me
+
     scratch = [
         pltpu.VMEM((R * rb, bsz), F32),
         pltpu.VMEM((up(R * nbd, bsz), bsz), F32),
@@ -283,37 +323,42 @@
             jax.ShapeDtypeStruct((cb, bsz), F32),
             jax.ShapeDtypeStruct((ndev, hp, bsz), F32),
         ),
-        in_specs=[VMEM] * (1 + R + 3) + [SMEM],
+        in_specs=[VMEM] * (2 + R),
         out_specs=(VMEM,) * 4,
         scratch_shapes=scratch,
         compiler_params=params,
         name="primal",
-    )(g1, *slots, x2, cost2, upper2, steps)
+    )(g1, *slots, aux)
     g3 = spread(p3)
     y_new, p4, dual = pl.pallas_call(
         functools.partial(dual_kernel, nbd, R, C, origins),
         out_shape=(
             jax.ShapeDtypeStruct((rb, bsz), F32),
             jax.ShapeDtypeStruct((C, bsz), F32),
-            jax.ShapeDtypeStruct((4, bsz), F32),
-        ),
-        in_specs=[VMEM] * (2 + R + 3) + [SMEM] + [VMEM] * 3,
+            jax.ShapeDtypeStruct((8, bsz), F32),
+        ),
+        in_specs=[VMEM] * (2 + R + 4),
         out_specs=(VMEM,) * 3,
         scratch_shapes=scratch,
         compiler_params=params,
         name="dual",
-    )(g1, g3, *slots, x2, cost2, upper2, steps, x_new, dr, dc)
+    )(g1, g3, *slots, aux, x_new, dr, dc)
     g4 = lax.all_to_all(p4, "col", 0, 0, tiled=True)
-    stats = pl.pallas_call(
+    stats, x_new, y_new = pl.pallas_call(
         functools.partial(
             stats_kernel, float(y_prev.shape[0] * R), float(x_prev.shape[0] * C)
         ),
-        out_shape=jax.ShapeDtypeStruct((1, 3), F32),
-        in_specs=[VMEM, VMEM, SMEM],
-        out_specs=VMEM,
+        out_shape=(
+            jax.ShapeDtypeStruct((1, 3), F32),
+            jax.ShapeDtypeStruct((cb, bsz), F32),
+            jax.ShapeDtypeStruct((rb, bsz), F32),
+        ),
+        in_specs=[VMEM] * 4,
+        out_specs=(VMEM, HBM, HBM),
+        scratch_shapes=[pltpu.SemaphoreType.DMA((2,))],
         compiler_params=params,
         name="stats",
-    )(g4, dual, steps)
+    )(g4, dual, x_new, y_new)
     return (x_new.reshape(-1), y_new.reshape(-1), stats.reshape(-1))
 
 

time: 55.7 us -> 43.9 us (0.79)
  blocking collectives: 33.3 us -> 19.6 us
  starting transfers between devices: 3.01 us -> 8.35 us
  local copies, waits for them, and re-layouts: 4.39 us -> 0 us
  waiting for transfers between devices: 7.1 us -> 8.9 us
  Pallas kernels: 6.1 us -> 5.43 us
    all_to_all x2 -> x1, blocking collectives: 23.7 us -> 10 us  [spread(): return lax.all_to_all(v, ('row', 'col'), 0, 0, tiled=True)]
    all_to_all x0 -> x1, waiting for transfers between devices: none -> 7.42 us  [spread(): return lax.all_to_all(v, ('row', 'col'), 0, 0, tiled=True)]
    ppermute x3, waiting for transfers between devices: 7.1 us -> 1.48 us  [shards(): slots += [lax.ppermute(b, 'row', perm) for b in slots]]
    all_to_all x0 -> x1, starting transfers between devices: none -> 4.92 us  [spread(): return lax.all_to_all(v, ('row', 'col'), 0, 0, tiled=True)]
    unnamed x20 -> x0, local copies, waits for them, and re-layouts: 4.39 us -> none
    pallas_call x1, Pallas kernels: 0.73 us -> 2.06 us  [shards(): pl.pallas_call(functools.partial(peaks_kernel, nbd), out_shape=(jax.Shape...]
    pallas_call x1, Pallas kernels: 2.14 us -> 1.13 us  [shards(): pl.pallas_call(functools.partial(dual_kernel, nbd, R, C, origins), out_sh...]
    pallas_call x1, Pallas kernels: 2.09 us -> 1.1 us  [shards(): pl.pallas_call(functools.partial(primal_kernel, nbd, R, C, origins), out_...]
  transfers between devices with their start and end apart: 3 -> 4, of which waited for: 1 -> 2; matrix products, arithmetic and copies ran while one was open for 0% -> 0% of each run, Pallas kernels for 0% -> 0%
where the time goes in v2:
time: 43.9 us; the launch traced here: 43.6 us
  blocking collectives  19.6 us (45%)
  waiting for transfers between devices  8.9 us (20%)
  starting transfers between devices  8.35 us (19%)
  Pallas kernels  5.43 us (12%)
  between operations  1.31 us (3%)
    all_to_all x1, blocking collectives, spread(): return lax.all_to_all(v, ('row', 'col'), 0, 0, tiled=True)  10 us
    all_to_all x1, blocking collectives, shards(): g4 = lax.all_to_all(p4, 'col', 0, 0, tiled=True)  9.58 us
    all_to_all x1, waiting for transfers between devices, spread(): return lax.all_to_all(v, ('row', 'col'), 0, 0, tiled=True)  7.42 us
    all_to_all x1, starting transfers between devices, spread(): return lax.all_to_all(v, ('row', 'col'), 0, 0, tiled=True)  4.92 us
    ppermute x3, starting transfers between devices, shards(): slots += [lax.ppermute(b, 'row', perm) for b in slots]  3.43 us
    pallas_call x1, Pallas kernels, shards(): pl.pallas_call(functools.partial(peaks_kernel, nbd), out_shape=(jax.Shape...  2.06 us
    ppermute x3, waiting for transfers between devices, shards(): slots += [lax.ppermute(b, 'row', perm) for b in slots]  1.48 us
    pallas_call x1, Pallas kernels, shards(): pl.pallas_call(functools.partial(stats_kernel, float(y_prev.shape[0] * R)...  1.14 us
  transfers between devices with their start and end apart: 4, of which 2 were waited for; matrix products, arithmetic and copies ran while one was open for 0% of the time, Pallas kernels for 0%

profile of v2, /device:TPU:0, one launch (start us, length us, event | category | flops | bytes accessed | tf_op | source)
XLA Modules:
  0.0 43.6 jit_solution(913054918375633833)
XLA Ops:
  1.3 2.1 %peaks.1 = (f32[32,8,128]{2,1,0:T(8,128)}, f32[584,128]{1,0:T(8,128)S(1)}, f32[32,128]{1,0:T(8,128)S(1)}) custom-call(f32[4,128,128]{2,1,0:T(8,128)} %bitcast.15, f32[32,128]{1,0:T(8,128)} %bitcast.16, f32[32,128]{1,0:T(8,128)} %bitcast.17, f32[8,128]{1,0:T(8,128)} %bitcast.18, f32[8,128]{1,0:T(8,128)} %bitcast.19, f32[8,128]{1,0:T(8,128)} %bitcast.20, ...), custom_call_target="tpu_custom_call" | custom-call | tf_op jit(solution)/shard_map/peaks/pallas_call | solution.py:270
  3.4 3.0 %collective-permute-start = (f32[584,128]{1,0:T(8,128)S(1)}, f32[584,128]{1,0:T(8,128)S(1)}, u32[]{:S(2)}, u32[]{:S(2)}) collective-permute-start(f32[584,128]{1,0:T(8,128)S(1)} %get-tuple-element.19.refs_0_), channel_id=1, source_target_pairs={{0,16},{8,24},{16,0},{24,8},{1,17},{9,25},{17,1},{25,9},{2,18},{10... | collective-permute-start | bytes 897032 | tf_op jit(solution)/shard_map/ppermute | solution.py:303
  6.4 4.9 %all-to-all-start = ((f32[32,8,128]{2,1,0:T(8,128)}), f32[32,8,128]{2,1,0:T(8,128)S(1)}, u32[]{:S(2)}, u32[]{:S(2)}) async-start(f32[32,8,128]{2,1,0:T(8,128)} %get-tuple-element.18), calls=%async_computation | async-start | bytes 262144 | tf_op jit(solution)/shard_map/all_to_all | solution.py:296
  11.3 0.3 collective-permute-start.1
  11.6 7.4 %all-to-all-done.g1 = f32[32,8,128]{2,1,0:T(8,128)S(1)} async-done(((f32[32,8,128]{2,1,0:T(8,128)}), f32[32,8,128]{2,1,0:T(8,128)S(1)}, u32[]{:S(2)}, u32[]{:S(2)}) %all-to-all-start) | async-done | bytes 131104 | tf_op jit(solution)/shard_map/all_to_all | solution.py:296
  19.0 0.0 collective-permute-done.refs_1_
  19.0 0.1 collective-permute-start.2
  19.1 0.0 collective-permute-done.1.refs_2_
  19.1 1.5 %collective-permute-done.2.refs_3_ = f32[584,128]{1,0:T(8,128)S(1)} collective-permute-done((f32[584,128]{1,0:T(8,128)S(1)}, f32[584,128]{1,0:T(8,128)S(1)}, u32[]{:S(2)}, u32[]{:S(2)}) %collective-permute-start.2) | collective-permute-done | bytes 299040 | tf_op jit(solution)/shard_map/ppermute | solution.py:303
  20.6 1.1 %primal.1 = (f32[8,128]{1,0:T(8,128)S(1)}, f32[128,128]{1,0:T(8,128)S(1)}, f32[8,128]{1,0:T(8,128)S(1)}, f32[32,8,128]{2,1,0:T(8,128)S(1)}) custom-call(f32[32,8,128]{2,1,0:T(8,128)S(1)} %all-to-all-done.g1, f32[584,128]{1,0:T(8,128)S(1)} %get-tuple-element.19.refs_0_, f32[584,128]{1,0:T(8,128)S(1)} %collective-permute-done.refs_1_, ...), custom_call_target="tpu_custom_call" | custom-call | tf_op jit(solution)/shard_map/primal/pallas_call | solution.py:318
  21.7 10.0 %all_to_all.21.g3 = f32[32,8,128]{2,1,0:T(8,128)S(1)} all-to-all(f32[32,8,128]{2,1,0:T(8,128)S(1)} %get-tuple-element.23), channel_id=1, replica_groups=mesh['row'=4,'col'=8] {'row','col'}, dimensions={0} | all-to-all | bytes 262144 | tf_op jit(solution)/shard_map/all_to_all | solution.py:296
  31.7 1.1 %dual.1 = (f32[32,128]{1,0:T(8,128)S(1)}, f32[8,128]{1,0:T(8,128)S(1)}, f32[8,128]{1,0:T(8,128)S(1)}) custom-call(f32[32,8,128]{2,1,0:T(8,128)S(1)} %all-to-all-done.g1, f32[32,8,128]{2,1,0:T(8,128)S(1)} %all_to_all.21.g3, f32[584,128]{1,0:T(8,128)S(1)} %get-tuple-element.19.refs_0_, f32[584,128]{1,0:T(8,128)S(1)} %collective-permute-done.refs_1_, ...), custom_call_target="tpu_custom_call" | custom-call | tf_op jit(solution)/shard_map/dual/pallas_call | solution.py:333
  32.9 9.6 %all_to_all.22 = f32[8,1,128]{2,1,0:T(1,128)S(1)} all-to-all(f32[8,1,128]{2,1,0:T(1,128)S(1)} %bitcast.14), channel_id=1, replica_groups=mesh['row'=4,'col'=8] {'col'}, dimensions={0} | all-to-all | bytes 8192 | tf_op jit(solution)/shard_map/all_to_all | solution.py:346
  42.4 1.1 %stats.1 = (f32[1,3]{1,0:T(1,128)}, f32[8,128]{1,0:T(8,128)}, f32[32,128]{1,0:T(8,128)}) custom-call(f32[8,128]{1,0:T(8,128)S(1)} %bitcast.13, f32[8,128]{1,0:T(8,128)S(1)} %get-tuple-element.28.dual, f32[8,128]{1,0:T(8,128)S(1)} %get-tuple-element.24.refs_5_.x_new, f32[32,128]{1,0:T(8,128)S(1)} %get-tuple-element.29.y_new), custom_call_target="tpu_custom_call" | custom-call | tf_op jit(solution)/shard_map/stats/pallas_call | solution.py:347
Async XLA Ops:
  3.4 15.7 %collective-permute-start = (f32[584,128]{1,0:T(8,128)S(1)}, f32[584,128]{1,0:T(8,128)S(1)}, u32[]{:S(2)}, u32[]{:S(2)}) collective-permute-start(f32[584,128]{1,0:T(8,128)S(1)} %get-tuple-element.19.refs_0_), channel_id=1, source_target_pairs={{0,16},{8,24},{16,0},{24,8},{1,17},{9,25},{17,1},{25,9},{2,18},{10... | collective-permute-start | bytes 897032 | tf_op jit(solution)/shard_map/ppermute | solution.py:303
  6.4 12.7 %all-to-all-start = ((f32[32,8,128]{2,1,0:T(8,128)}), f32[32,8,128]{2,1,0:T(8,128)S(1)}, u32[]{:S(2)}, u32[]{:S(2)}) async-start(f32[32,8,128]{2,1,0:T(8,128)} %get-tuple-element.18), calls=%async_computation | async-start | bytes 262144 | tf_op jit(solution)/shard_map/all_to_all | solution.py:296
  11.3 7.9 %collective-permute-start.1 = (f32[584,128]{1,0:T(8,128)S(1)}, f32[584,128]{1,0:T(8,128)S(1)}, u32[]{:S(2)}, u32[]{:S(2)}) collective-permute-start(f32[584,128]{1,0:T(8,128)S(1)} %get-tuple-element.19.refs_0_), channel_id=1, source_target_pairs={{0,8},{8,0},{16,24},{24,16},{1,9},{9,1},{17,25},{25,17},{2,10},{10... | collective-permute-start | bytes 897032 | tf_op jit(solution)/shard_map/ppermute | solution.py:303
  19.0 1.6 %collective-permute-start.2 = (f32[584,128]{1,0:T(8,128)S(1)}, f32[584,128]{1,0:T(8,128)S(1)}, u32[]{:S(2)}, u32[]{:S(2)}) collective-permute-start(f32[584,128]{1,0:T(8,128)S(1)} %collective-permute-done.refs_1_), channel_id=1, source_target_pairs={{0,8},{8,0},{16,24},{24,16},{1,9},{9,1},{17,25},{25,17},{2,10},{10... | collective-permute-start | bytes 897032 | tf_op jit(solution)/shard_map/ppermute | solution.py:303

commit v3 on v2

v3 whole, which is shorter than its diff:
```python
import functools

import jax
import jax.numpy as jnp
from jax import lax
from jax.experimental import pallas as pl
from jax.experimental.pallas import tpu as pltpu
from jax.sharding import PartitionSpec as P

F32 = jnp.float32
VMEM = pl.BlockSpec(memory_space=pltpu.VMEM)
SMEM = pl.BlockSpec(memory_space=pltpu.SMEM)
HBM = pl.BlockSpec(memory_space=pltpu.HBM)
LIMIT = 40 * 1024 * 1024


def up(n, m):
    return -(-n // m) * m


def iota(shape, dim):
    return lax.broadcasted_iota(jnp.int32, shape, dim)


def rows_of(vectors, bsz):
    lane = iota((bsz, bsz), 1)
    cols = jnp.zeros((bsz, bsz), F32)
    for k, col in enumerate(vectors):
        cols = jnp.where(lane == k, col, cols)
    return cols.T


def total(rows):
    return jnp.sum(rows, axis=0, keepdims=True)


def peaks_kernel(nbd, blocks, y, rhs, x, cost, upper, brow, bcol, steps, count, p1, bulk, aux, *scratch):
    s_row, s_col, s_steps, sems = scratch
    bsz = bulk.shape[1]
    rb = y.shape[0]
    cb = x.shape[0]
    base = nbd * bsz
    pairs = [
        (brow, s_row),
        (bcol, s_col),
        (steps, s_steps),
        (y, bulk.at[base : base + rb]),
        (rhs, bulk.at[base + rb : base + 2 * rb]),
        (x, aux.at[:cb]),
        (cost, aux.at[cb : 2 * cb]),
        (upper, aux.at[2 * cb : 3 * cb]),
    ]
    loads = [
        pltpu.make_async_copy(blocks.at[k], bulk.at[k * bsz : (k + 1) * bsz], sems.at[k])
        for k in range(nbd)
    ]
    rest = [pltpu.make_async_copy(a, b, sems.at[nbd + i]) for i, (a, b) in enumerate(pairs)]
    for copy in loads + rest:
        copy.start()
    peaks = []
    for k in range(nbd):
        loads[k].wait()
        a = bulk[k * bsz : (k + 1) * bsz, :]
        peaks.append(jnp.max(jnp.abs(a), axis=1, keepdims=True))
    rows = rows_of(peaks, bsz)
    for copy in rest:
        copy.wait()
    lane = iota((1, bsz), 1)
    meta = jnp.full((1, bsz), -1.0, F32)
    for k in range(nbd):
        code = jnp.where(k < count[0, 0], s_row[0, 0, k], -1).astype(F32)
        meta = jnp.where(lane == k, code, meta)
        meta = jnp.where(lane == nbd + k, s_col[0, 0, k].astype(F32), meta)
    pieces = [rows[k : k + 1, :] for k in range(nbd)] + [meta]
    for k, piece in enumerate(pieces):
        p1[:, :, k * bsz : (k + 1) * bsz] = jnp.broadcast_to(piece[None], (p1.shape[0], 1, bsz))
    asub = iota((8, bsz), 0)
    aux[3 * cb :, :] = jnp.where(asub == 0, s_steps[0], s_steps[1])


def backward(nbd, rb, cb, q, slot, codes, w_ref, wr):
    me_c = lax.axis_index("col")
    bsz = slot.shape[1]
    rio = iota((rb, bsz), 0).astype(F32)
    cio = iota((cb, bsz), 0).astype(F32)
    w = w_ref[pl.ds(pl.multiple_of(q * rb, rb), rb), :]
    for k in range(nbd):
        hit = rio == codes[q, k, pl.ds(me_c, 1), :]
        wr[k : k + 1, :] = total(jnp.where(hit, w, 0.0))
    wt = wr[...].T
    out = jnp.zeros((cb, bsz), F32)
    for k in range(nbd):
        prod = total(slot[k * bsz : (k + 1) * bsz, :] * wt[:, k : k + 1])
        out += jnp.where(cio == codes[q, nbd + k, pl.ds(me_c, 1), :], prod, 0.0)
    return out


def col_peaks(nbd, cb, q, slot, codes):
    me_c = lax.axis_index("col")
    bsz = slot.shape[1]
    cio = iota((cb, bsz), 0).astype(F32)
    out = jnp.zeros((cb, bsz), F32)
    for k in range(nbd):
        peak = jnp.max(jnp.abs(slot[k * bsz : (k + 1) * bsz, :]), axis=0, keepdims=True)
        live = codes[q, k, pl.ds(me_c, 1), :] >= 0.0
        hit = (cio == codes[q, nbd + k, pl.ds(me_c, 1), :]) & live
        out = jnp.maximum(out, jnp.where(hit, peak, 0.0))
    return out


def scales_kernel(nbd, R, C, rb, cb, origins, g1, *refs):
    half = max(R // 2, 1)
    slots = refs[:half]
    dr, codes, part, colmax, w_ref, wr = refs[half:]
    me_r = lax.axis_index("row")
    bsz = dr.shape[1]
    base = nbd * bsz
    rio = iota((rb, bsz), 0).astype(F32)
    wr[...] = jnp.zeros_like(wr)
    for q in range(R):
        meta = g1[q * C : (q + 1) * C, 0, base:]
        for k in range(2 * nbd):
            codes[q, k] = jnp.broadcast_to(meta[:, k : k + 1], (C, bsz))

        def body(c, acc):
            for k in range(nbd):
                hit = rio == codes[q, k, pl.ds(c, 1), :]
                acc = jnp.maximum(acc, jnp.where(hit, g1[q * C + c, :, k * bsz : (k + 1) * bsz], 0.0))
            return acc

        peak = lax.fori_loop(0, C, body, jnp.zeros((rb, bsz), F32), unroll=min(C, 8))
        dr[q * rb : (q + 1) * rb, :] = 1.0 / jnp.sqrt(jnp.maximum(peak, 0.5))
    top = jnp.zeros((cb, bsz), F32)
    for s, slot in enumerate(slots):
        q = origins(me_r, s)
        at = pl.ds(pl.multiple_of(q * rb, rb), rb)
        w_ref[at, :] = dr[at, :] * slot[base : base + rb, :]
        top = jnp.maximum(top, col_peaks(nbd, cb, q, slot, codes))
        part[q] = backward(nbd, rb, cb, q, slot, codes, w_ref, wr)
    colmax[...] = top


def primal_kernel(nbd, R, C, rb, cb, origins, *refs):
    half = max(R // 2, 1)
    slots, own = refs[: R - half], refs[R - half]
    aux, dr, codes, done, colmax, x_new, dc, p3, w_ref, wr, part = refs[R - half + 1 :]
    me_r = lax.axis_index("row")
    me_c = lax.axis_index("col")
    bsz = x_new.shape[1]
    base = nbd * bsz
    x_prev, cost, upper = (aux[i * cb : (i + 1) * cb, :] for i in range(3))
    eta, omega = (aux[3 * cb + i : 3 * cb + i + 1, :] for i in range(2))
    cio = iota((cb, bsz), 0).astype(F32)
    wr[...] = jnp.zeros_like(wr)
    top = colmax[...]
    for s in range(half):
        q = origins(me_r, s)
        part[q] = done[q]
    for s, slot in enumerate(slots):
        q = origins(me_r, half + s)
        at = pl.ds(pl.multiple_of(q * rb, rb), rb)
        w_ref[at, :] = dr[at, :] * slot[base : base + rb, :]
        top = jnp.maximum(top, col_peaks(nbd, cb, q, slot, codes))
        part[q] = backward(nbd, rb, cb, q, slot, codes, w_ref, wr)
    got = part[0]
    for q in range(1, R):
        got += part[q]
    scale = 1.0 / jnp.sqrt(jnp.maximum(top, 0.5))
    dc[...] = scale
    grad = scale * cost - got * scale
    xn = jnp.clip(x_prev - eta / omega * grad, 0.0, upper / scale)
    x_new[...] = xn
    v1 = scale * xn
    v2 = scale * (xn - x_prev)
    res = []
    for k in range(nbd):
        a = own[k * bsz : (k + 1) * bsz, :]
        hit = cio == codes[me_r, nbd + k, pl.ds(me_c, 1), :]
        for v in (v1, v2):
            res.append(jnp.sum(a * total(jnp.where(hit, v, 0.0)), axis=1, keepdims=True))
    rows = rows_of(res, bsz)[: p3.shape[1]]
    p3[...] = jnp.broadcast_to(rows[None], p3.shape)


def dual_kernel(nbd, R, C, rb, cb, origins, g3, *refs):
    slots = refs[:R]
    aux, dr, codes, x_new, dc, y_new, p4, dual, w_ref, wr, part = refs[R:]
    me_r = lax.axis_index("row")
    bsz = x_new.shape[1]
    base = nbd * bsz
    x_prev, cost, upper = (aux[i * cb : (i + 1) * cb, :] for i in range(3))
    eta, omega = (aux[3 * cb + i : 3 * cb + i + 1, :] for i in range(2))
    rio = iota((rb, bsz), 0).astype(F32)
    wr[...] = jnp.zeros_like(wr)
    sigma = eta * omega
    for s, slot in enumerate(slots):
        q = origins(me_r, s)
        at = pl.ds(pl.multiple_of(q * rb, rb), rb)

        def body(c, acc):
            one, two = acc
            got = g3[q * C + c]
            for k in range(nbd):
                hit = rio == codes[q, k, pl.ds(c, 1), :]
                one = one + jnp.where(hit, got[2 * k : 2 * k + 1, :], 0.0)
                two = two + jnp.where(hit, got[2 * k + 1 : 2 * k + 2, :], 0.0)
            return one, two

        zero = jnp.zeros((rb, bsz), F32)
        ax, adx = lax.fori_loop(0, C, body, (zero, zero), unroll=min(C, 8))
        scale = dr[at, :]
        ax = ax * scale
        adx = adx * scale
        bs = scale * slot[base + rb : base + 2 * rb, :]
        yp = slot[base : base + rb, :]
        yn = yp + sigma * (bs - ax - adx)
        if s == 0:
            y_new[...] = yn
        w_ref[at, :] = scale * yn
        dy = yn - yp
        resid = bs - ax
        for i, term in enumerate((dy * dy, adx * adx, resid * resid, bs * yn)):
            part[q, i : i + 1, :] = total(term)
    sums = part[0, :4, :]
    for q in range(1, R):
        sums += part[q, :4, :]
    dual[:4, :] = jnp.broadcast_to(jnp.sum(sums, axis=1, keepdims=True), (4, bsz))
    dual[4:, :] = jnp.broadcast_to(omega, (4, bsz))
    for s, slot in enumerate(slots):
        q = origins(me_r, s)
        part[q] = backward(nbd, rb, cb, q, slot, codes, w_ref, wr)
    got = part[0]
    for q in range(1, R):
        got += part[q]
    scale = dc[...]
    cs = scale * cost
    reduced = cs - got * scale
    us = upper / scale
    xn = x_new[...]
    dx = xn - x_prev
    lane = iota((1, bsz), 1)
    out = jnp.zeros((1, bsz), F32)
    for i, term in enumerate((dx * dx, cs * xn, us * jnp.maximum(-reduced, 0.0))):
        out = jnp.where(lane == i, jnp.sum(term), out)
    p4[...] = jnp.broadcast_to(out[None], p4.shape)


def stats_kernel(C, total_rows, total_cols, g4, dual, x_new, y_new, stats, x_out, y_out, sems):
    outs = [
        pltpu.make_async_copy(x_new, x_out, sems.at[0]),
        pltpu.make_async_copy(y_new, y_out, sems.at[1]),
    ]
    for copy in outs:
        copy.start()
    bsz = g4.shape[2]
    primal = g4[0]
    for c in range(1, C):
        primal += g4[c]
    lane = iota((1, bsz), 1)

    def pick(i):
        return jnp.sum(jnp.where(lane == i, primal, 0.0), axis=1, keepdims=True)

    dx2, cx, uneg = (jnp.broadcast_to(pick(i), (1, bsz)) for i in range(3))
    dy2, adx2, res2, by = (dual[i : i + 1, :] for i in range(4))
    omega = dual[4:5, :]
    movement = 0.5 * omega * dx2 + 0.5 / omega * dy2
    first = jnp.sqrt(res2 / total_rows)
    second = (cx - by + uneg) / total_cols
    third = movement / jnp.sqrt(adx2 * dy2 + 1e-06)
    out = jnp.where(lane == 0, first, jnp.where(lane == 1, second, third))
    stats[...] = out[:, : stats.shape[1]]
    for copy in outs:
        copy.wait()


def shards(blocks, block_rows, block_cols, counts, x_prev, y_prev, cost, rhs, upper, steps):
    R = lax.axis_size("row")
    C = lax.axis_size("col")
    ndev = R * C
    nbd, bsz = blocks.shape[2], blocks.shape[3]
    rb = y_prev.shape[0] // bsz
    cb = x_prev.shape[0] // bsz
    half = max(R // 2, 1)
    shape = lambda *dims: jax.ShapeDtypeStruct(dims, F32)
    params = pltpu.CompilerParams(vmem_limit_bytes=LIMIT)
    raw = (
        blocks[0, 0],
        y_prev.reshape(rb, bsz),
        rhs.reshape(rb, bsz),
        x_prev.reshape(cb, bsz),
        cost.reshape(cb, bsz),
        upper.reshape(cb, bsz),
        block_rows,
        block_cols,
        steps,
    )
    p1, bulk, aux = pl.pallas_call(
        functools.partial(peaks_kernel, nbd),
        out_shape=(
            shape(ndev, 1, (nbd + 1) * bsz),
            shape(nbd * bsz + 2 * rb, bsz),
            shape(3 * cb + 8, bsz),
        ),
        in_specs=[HBM] * len(raw) + [SMEM],
        out_specs=(VMEM,) * 3,
        scratch_shapes=[
            pltpu.SMEM((1, 1, nbd), jnp.int32),
            pltpu.SMEM((1, 1, nbd), jnp.int32),
            pltpu.SMEM(steps.shape, F32),
            pltpu.SemaphoreType.DMA((nbd + 8,)),
        ],
        compiler_params=params,
        name="peaks",
    )(*(pltpu.with_memory_space_constraint(v, pltpu.HBM) for v in raw), counts)

    def spread(v):
        return lax.all_to_all(v, ("row", "col"), 0, 0, tiled=True)

    step = R // 2
    ids, slots = [0], [bulk]
    while step > 1:
        slots += [lax.ppermute(b, "row", [(i, i ^ step) for i in range(R)]) for b in slots]
        ids += [i ^ step for i in ids]
        step //= 2
    g1 = spread(p1)
    g1, bulk, *slots = lax.optimization_barrier((g1, bulk, *slots[1:]))
    slots = [bulk, *slots]
    if R > 1:
        slots += [lax.ppermute(b, "row", [(i, i ^ 1) for i in range(R)]) for b in slots]
        ids += [i ^ 1 for i in ids]

    def origins(me, s):
        return me ^ ids[s] if ids[s] else me

    scratch = [
        pltpu.VMEM((R * rb, bsz), F32),
        pltpu.VMEM((up(nbd, bsz), bsz), F32),
    ]
    part = pltpu.VMEM((R, up(cb, 8), bsz), F32)
    sizes = (nbd, R, C, rb, cb, origins)
    dr, codes, done, colmax = pl.pallas_call(
        functools.partial(scales_kernel, *sizes),
        out_shape=(
            shape(R * rb, bsz),
            shape(R, 2 * nbd, C, bsz),
            shape(R, cb, bsz),
            shape(cb, bsz),
        ),
        in_specs=[VMEM] * (1 + half),
        out_specs=(VMEM,) * 4,
        scratch_shapes=scratch,
        compiler_params=params,
        name="scales",
    )(g1, *slots[:half])
    x_new, dc, p3 = pl.pallas_call(
        functools.partial(primal_kernel, *sizes),
        out_shape=(shape(cb, bsz), shape(cb, bsz), shape(ndev, up(2 * nbd, 8), bsz)),
        in_specs=[VMEM] * (R - half + 6),
        out_specs=(VMEM,) * 3,
        scratch_shapes=scratch + [part],
        compiler_params=params,
        name="primal",
    )(*slots[half:], bulk, aux, dr, codes, done, colmax)
    g3 = spread(p3)
    y_new, p4, dual = pl.pallas_call(
        functools.partial(dual_kernel, *sizes),
        out_shape=(shape(rb, bsz), shape(ndev, 1, bsz), shape(8, bsz)),
        in_specs=[VMEM] * (R + 6),
        out_specs=(VMEM,) * 3,
        scratch_shapes=scratch + [part],
        compiler_params=params,
        name="dual",
    )(g3, *slots, aux, dr, codes, x_new, dc)
    g4 = spread(p4)
    stats, x_new, y_new = pl.pallas_call(
        functools.partial(
            stats_kernel, C, float(y_prev.shape[0] * R), float(x_prev.shape[0] * C)
        ),
        out_shape=(shape(1, 3), shape(cb, bsz), shape(rb, bsz)),
        in_specs=[VMEM] * 4,
        out_specs=(VMEM, HBM, HBM),
        scratch_shapes=[pltpu.SemaphoreType.DMA((2,))],
        compiler_params=params,
        name="stats",
    )(g4, dual, x_new, y_new)
    return (x_new.reshape(-1), y_new.reshape(-1), stats.reshape(-1))


def solution(mesh):
    placed = (
        P("row", "col", None, None, None),
        P("row", "col", None),
        P("row", "col", None),
        P("row", "col"),
        P("col"),
        P("row"),
        P("col"),
        P("row"),
        P("col"),
        P(),
    )
    return jax.shard_map(
        shards, mesh=mesh, in_specs=placed, out_specs=(P("col"), P("row"), P()), check_vma=False
    )
```

time: 43.9 us -> 41.8 us (0.952)
  blocking collectives: 19.6 us -> 30.9 us
  waiting for transfers between devices: 8.9 us -> 0.67 us
  starting transfers between devices: 8.35 us -> 3.51 us
    all_to_all x1 -> x3, blocking collectives: 10 us -> 30.9 us  [spread(): return lax.all_to_all(v, ('row', 'col'), 0, 0, tiled=True)]
    all_to_all x1 -> x0, blocking collectives: 9.58 us -> none  [shards(): g4 = lax.all_to_all(p4, 'col', 0, 0, tiled=True)]
    all_to_all x1 -> x0, waiting for transfers between devices: 7.42 us -> none  [spread(): return lax.all_to_all(v, ('row', 'col'), 0, 0, tiled=True)]
    all_to_all x1 -> x0, starting transfers between devices: 4.92 us -> none  [spread(): return lax.all_to_all(v, ('row', 'col'), 0, 0, tiled=True)]
    ppermute x3, waiting for transfers between devices: 1.48 us -> 0.67 us  [the longest x2 0.66 us: shards(): lax.ppermute(b, 'row', [(i, i ^ 1) for i in range(R)])]
    pallas_call x4 -> x5, Pallas kernels: 5.43 us -> 5.15 us  [the longest x1 1.44 us: shards(): pl.pallas_call(functools.partial(peaks_kernel, nbd), out_shape=(shape(nde...]
  transfers between devices with their start and end apart: 4 -> 3, of which waited for: 2 -> 2; matrix products, arithmetic and copies ran while one was open for 0% -> 0% of each run, Pallas kernels for 0% -> 2%
where the time goes in v3:
time: 41.8 us; the launch traced here: 41.5 us
  blocking collectives  30.9 us (74%)
  Pallas kernels  5.15 us (12%)
  starting transfers between devices  3.51 us (8%)
  between operations  1.31 us (3%)
  waiting for transfers between devices  0.67 us (2%)
    all_to_all x3, blocking collectives, spread(): return lax.all_to_all(v, ('row', 'col'), 0, 0, tiled=True)  30.9 us
    ppermute x1, starting transfers between devices, shards(): lax.ppermute(b, 'row', [(i, i ^ step) for i in range(R)])  3 us
    pallas_call x1, Pallas kernels, shards(): pl.pallas_call(functools.partial(peaks_kernel, nbd), out_shape=(shape(nde...  1.44 us
    pallas_call x1, Pallas kernels, shards(): pl.pallas_call(functools.partial(stats_kernel, C, float(y_prev.shape[0] *...  1.14 us
    pallas_call x1, Pallas kernels, shards(): pl.pallas_call(functools.partial(dual_kernel, *sizes), out_shape=(shape(r...  1.05 us
  transfers between devices with their start and end apart: 3, of which 2 were waited for; matrix products, arithmetic and copies ran while one was open for 0% of the time, Pallas kernels for 2%

profile of v3, /device:TPU:0, one launch (start us, length us, event | category | flops | bytes accessed | tf_op | source)
XLA Modules:
  0.0 41.5 jit_solution(12885679261144547088)
XLA Ops:
  1.3 1.4 %peaks.1 = (f32[32,1,640]{2,1,0:T(1,128)S(1)}, f32[576,128]{1,0:T(8,128)S(1)}, f32[32,128]{1,0:T(8,128)S(1)}) custom-call(f32[4,128,128]{2,1,0:T(8,128)} %bitcast.9, f32[32,128]{1,0:T(8,128)} %bitcast.10, f32[32,128]{1,0:T(8,128)} %bitcast.11, f32[8,128]{1,0:T(8,128)} %bitcast.12, f32[8,128]{1,0:T(8,128)} %bitcast.13, f32[8,128]{1,0:T(8,128)} %bitcast.14, ...), custom_call_target="tpu_custom_call" | custom-call | tf_op jit(solution)/shard_map/peaks/pallas_call | solution.py:298
  2.7 3.0 %collective-permute-start = (f32[576,128]{1,0:T(8,128)S(1)}, f32[576,128]{1,0:T(8,128)S(1)}, u32[]{:S(2)}, u32[]{:S(2)}) collective-permute-start(f32[576,128]{1,0:T(8,128)S(1)} %get-tuple-element.24.refs_0_.refs_2_), channel_id=1, source_target_pairs={{0,16},{8,24},{16,0},{24,8},{1,17},{9,25},{17,1},{25,9},{2,18},{10... | collective-permute-start | bytes 884744 | tf_op jit(solution)/shard_map/ppermute | solution.py:323
  5.7 12.2 %all_to_all.15.g1 = f32[32,1,640]{2,1,0:T(1,128)S(1)} all-to-all(f32[32,1,640]{2,1,0:T(1,128)S(1)} %get-tuple-element.22), channel_id=1, replica_groups=mesh['row'=4,'col'=8] {'row','col'}, dimensions={0} | all-to-all | bytes 163840 | tf_op jit(solution)/shard_map/all_to_all | solution.py:318
  17.9 0.0 collective-permute-done.refs_1_
  17.9 0.1 collective-permute-start.2
  18.0 0.4 collective-permute-start.1
  18.4 0.8 %scales.1 = (f32[128,128]{1,0:T(8,128)S(1)}, f32[4,8,8,128]{3,2,1,0:T(8,128)S(1)}, f32[4,8,128]{2,1,0:T(8,128)S(1)}, f32[8,128]{1,0:T(8,128)S(1)}) custom-call(f32[32,1,640]{2,1,0:T(1,128)S(1)} %all_to_all.15.g1, f32[576,128]{1,0:T(8,128)S(1)} %get-tuple-element.24.refs_0_.refs_2_, f32[576,128]{1,0:T(8,128)S(1)} %collective-permute-done.refs_1_), custom_call_target="tpu_custom_call" | custom-call | tf_op jit(solution)/shard_map/scales/pallas_call | solution.py:342
  19.2 0.2 collective-permute-done.2.refs_1_.refs_3_
  19.5 0.4 %collective-permute-done.1.refs_0_.refs_2_ = f32[576,128]{1,0:T(8,128)S(1)} collective-permute-done((f32[576,128]{1,0:T(8,128)S(1)}, f32[576,128]{1,0:T(8,128)S(1)}, u32[]{:S(2)}, u32[]{:S(2)}) %collective-permute-start.1) | collective-permute-done | bytes 294944 | tf_op jit(solution)/shard_map/ppermute | solution.py:330
  19.9 0.7 %primal.1 = (f32[8,128]{1,0:T(8,128)S(1)}, f32[8,128]{1,0:T(8,128)S(1)}, f32[32,8,128]{2,1,0:T(8,128)S(1)}) custom-call(f32[576,128]{1,0:T(8,128)S(1)} %collective-permute-done.1.refs_0_.refs_2_, f32[576,128]{1,0:T(8,128)S(1)} %collective-permute-done.2.refs_1_.refs_3_, f32[576,128]{1,0:T(8,128)S(1)} %get-tuple-element.24.refs_0_.refs_2_, ...), custom_call_target="tpu_custom_call" | custom-call | tf_op jit(solution)/shard_map/primal/pallas_call | solution.py:356
  20.6 9.4 %all_to_all.16.g3 = f32[32,8,128]{2,1,0:T(8,128)S(1)} all-to-all(f32[32,8,128]{2,1,0:T(8,128)S(1)} %get-tuple-element.32), channel_id=1, replica_groups=mesh['row'=4,'col'=8] {'row','col'}, dimensions={0} | all-to-all | bytes 262144 | tf_op jit(solution)/shard_map/all_to_all | solution.py:318
  30.0 1.1 %dual.1 = (f32[32,128]{1,0:T(8,128)S(1)}, f32[32,1,128]{2,1,0:T(1,128)S(1)}, f32[8,128]{1,0:T(8,128)S(1)}) custom-call(f32[32,8,128]{2,1,0:T(8,128)S(1)} %all_to_all.16.g3, f32[576,128]{1,0:T(8,128)S(1)} %get-tuple-element.24.refs_0_.refs_2_, f32[576,128]{1,0:T(8,128)S(1)} %collective-permute-done.refs_1_, ...), custom_call_target="tpu_custom_call" | custom-call | tf_op jit(solution)/shard_map/dual/pallas_call | solution.py:366
  31.1 9.3 %all_to_all.17.g4 = f32[32,1,128]{2,1,0:T(1,128)S(1)} all-to-all(f32[32,1,128]{2,1,0:T(1,128)S(1)} %get-tuple-element.35), channel_id=1, replica_groups=mesh['row'=4,'col'=8] {'row','col'}, dimensions={0} | all-to-all | bytes 32768 | tf_op jit(solution)/shard_map/all_to_all | solution.py:318
  40.4 1.1 %stats.1 = (f32[1,3]{1,0:T(1,128)}, f32[8,128]{1,0:T(8,128)}, f32[32,128]{1,0:T(8,128)}) custom-call(f32[32,1,128]{2,1,0:T(1,128)S(1)} %all_to_all.17.g4, f32[8,128]{1,0:T(8,128)S(1)} %get-tuple-element.36.dual, f32[8,128]{1,0:T(8,128)S(1)} %get-tuple-element.33.refs_7_.x_new, f32[32,128]{1,0:T(8,128)S(1)} %get-tuple-element.37.y_new), custom_call_target="tpu_custom_call" | custom-call | tf_op jit(solution)/shard_map/stats/pallas_call | solution.py:376
Async XLA Ops:
  2.7 15.2 %collective-permute-start = (f32[576,128]{1,0:T(8,128)S(1)}, f32[576,128]{1,0:T(8,128)S(1)}, u32[]{:S(2)}, u32[]{:S(2)}) collective-permute-start(f32[576,128]{1,0:T(8,128)S(1)} %get-tuple-element.24.refs_0_.refs_2_), channel_id=1, source_target_pairs={{0,16},{8,24},{16,0},{24,8},{1,17},{9,25},{17,1},{25,9},{2,18},{10... | collective-permute-start | bytes 884744 | tf_op jit(solution)/shard_map/ppermute | solution.py:323
  17.9 1.6 %collective-permute-start.2 = (f32[576,128]{1,0:T(8,128)S(1)}, f32[576,128]{1,0:T(8,128)S(1)}, u32[]{:S(2)}, u32[]{:S(2)}) collective-permute-start(f32[576,128]{1,0:T(8,128)S(1)} %collective-permute-done.refs_1_), channel_id=1, source_target_pairs={{0,8},{8,0},{16,24},{24,16},{1,9},{9,1},{17,25},{25,17},{2,10},{10... | collective-permute-start | bytes 884744 | tf_op jit(solution)/shard_map/ppermute | solution.py:330
  18.0 1.9 %collective-permute-start.1 = (f32[576,128]{1,0:T(8,128)S(1)}, f32[576,128]{1,0:T(8,128)S(1)}, u32[]{:S(2)}, u32[]{:S(2)}) collective-permute-start(f32[576,128]{1,0:T(8,128)S(1)} %get-tuple-element.24.refs_0_.refs_2_), channel_id=1, source_target_pairs={{0,8},{8,0},{16,24},{24,16},{1,9},{9,1},{17,25},{25,17},{2,10},{10... | collective-permute-start | bytes 884744 | tf_op jit(solution)/shard_map/ppermute | solution.py:330

commit v4 on v3

--- a/solution.py
+++ b/solution.py
@@ -109,9 +109,9 @@
 
 
 def scales_kernel(nbd, R, C, rb, cb, origins, g1, *refs):
-    half = max(R // 2, 1)
+    half = min(R, 2)
     slots = refs[:half]
-    dr, codes, part, colmax, w_ref, wr = refs[half:]
+    dr, codes, packed, part, colmax, w_ref, wr = refs[half:]
     me_r = lax.axis_index("row")
     bsz = dr.shape[1]
     base = nbd * bsz
@@ -130,6 +130,11 @@
 
         peak = lax.fori_loop(0, C, body, jnp.zeros((rb, bsz), F32), unroll=min(C, 8))
         dr[q * rb : (q + 1) * rb, :] = 1.0 / jnp.sqrt(jnp.maximum(peak, 0.5))
+    share = iota((C, bsz), 1) // (bsz // C)
+    mine = jnp.full((C, bsz), -1.0, F32)
+    for k in range(nbd):
+        mine = jnp.where(share == k, codes[me_r, k], mine)
+    packed[...] = mine
     top = jnp.zeros((cb, bsz), F32)
     for s, slot in enumerate(slots):
         q = origins(me_r, s)
@@ -141,7 +146,7 @@
 
 
 def primal_kernel(nbd, R, C, rb, cb, origins, *refs):
-    half = max(R // 2, 1)
+    half = min(R, 2)
     slots, own = refs[: R - half], refs[R - half]
     aux, dr, codes, done, colmax, x_new, dc, p3, w_ref, wr, part = refs[R - half + 1 :]
     me_r = lax.axis_index("row")
@@ -170,22 +175,35 @@
     grad = scale * cost - got * scale
     xn = jnp.clip(x_prev - eta / omega * grad, 0.0, upper / scale)
     x_new[...] = xn
-    v1 = scale * xn
     v2 = scale * (xn - x_prev)
-    res = []
+    v1 = scale * xn + v2
+    both, step = [], []
     for k in range(nbd):
         a = own[k * bsz : (k + 1) * bsz, :]
         hit = cio == codes[me_r, nbd + k, pl.ds(me_c, 1), :]
-        for v in (v1, v2):
-            res.append(jnp.sum(a * total(jnp.where(hit, v, 0.0)), axis=1, keepdims=True))
-    rows = rows_of(res, bsz)[: p3.shape[1]]
-    p3[...] = jnp.broadcast_to(rows[None], p3.shape)
+        for v, out in ((v1, both), (v2, step)):
+            out.append(jnp.sum(a * total(jnp.where(hit, v, 0.0)), axis=1, keepdims=True))
+    rows = rows_of(both + step, bsz)
+    lanes = bsz // C
+    share = iota((C, bsz), 1) // lanes
+    row = jnp.zeros((C, bsz), F32)
+    for k in range(nbd):
+        part_k = pltpu.roll(rows[nbd + k : nbd + k + 1, :], (k + 1) * lanes % bsz, 1)
+        part_k = jnp.broadcast_to(part_k, (C, bsz))
+        part_k = pltpu.roll(part_k, 0, 1, stride=lanes, stride_axis=0)
+        row = jnp.where(share == k, part_k, row)
+        p3[:, :, k * bsz : (k + 1) * bsz] = jnp.broadcast_to(
+            rows[k : k + 1, :][None], (p3.shape[0], 1, bsz)
+        )
+    for q in range(R):
+        p3[q * C : (q + 1) * C, 0, base:] = row
 
 
 def dual_kernel(nbd, R, C, rb, cb, origins, g3, *refs):
     slots = refs[:R]
-    aux, dr, codes, x_new, dc, y_new, p4, dual, w_ref, wr, part = refs[R:]
+    aux, dr, codes, packed, x_new, dc, y_new, p4, dual, w_ref, wr, part = refs[R:]
     me_r = lax.axis_index("row")
+    me_c = lax.axis_index("col")
     bsz = x_new.shape[1]
     base = nbd * bsz
     x_prev, cost, upper = (aux[i * cb : (i + 1) * cb, :] for i in range(3))
@@ -198,34 +216,44 @@
         at = pl.ds(pl.multiple_of(q * rb, rb), rb)
 
         def body(c, acc):
-            one, two = acc
-            got = g3[q * C + c]
             for k in range(nbd):
                 hit = rio == codes[q, k, pl.ds(c, 1), :]
-                one = one + jnp.where(hit, got[2 * k : 2 * k + 1, :], 0.0)
-                two = two + jnp.where(hit, got[2 * k + 1 : 2 * k + 2, :], 0.0)
-            return one, two
-
-        zero = jnp.zeros((rb, bsz), F32)
-        ax, adx = lax.fori_loop(0, C, body, (zero, zero), unroll=min(C, 8))
+                acc = acc + jnp.where(hit, g3[q * C + c, :, k * bsz : (k + 1) * bsz], 0.0)
+            return acc
+
+        both = lax.fori_loop(0, C, body, jnp.zeros((rb, bsz), F32), unroll=min(C, 8))
         scale = dr[at, :]
-        ax = ax * scale
-        adx = adx * scale
+        both = both * scale
         bs = scale * slot[base + rb : base + 2 * rb, :]
         yp = slot[base : base + rb, :]
-        yn = yp + sigma * (bs - ax - adx)
+        yn = yp + sigma * (bs - both)
+        w_ref[at, :] = scale * yn
+        dy = yn - yp
+        part[q, 0:1, :] = total(dy * dy)
+        part[q, 1:2, :] = total(bs * yn)
         if s == 0:
             y_new[...] = yn
-        w_ref[at, :] = scale * yn
-        dy = yn - yp
-        resid = bs - ax
-        for i, term in enumerate((dy * dy, adx * adx, resid * resid, bs * yn)):
-            part[q, i : i + 1, :] = total(term)
-    sums = part[0, :4, :]
+
+            def mine(c, acc):
+                hit = rio == packed[pl.ds(c, 1), :]
+                return acc + jnp.where(hit, g3[q * C + c, :, base:], 0.0)
+
+            shares = lax.fori_loop(0, C, mine, jnp.zeros((rb, bsz), F32), unroll=min(C, 8))
+            lanes = bsz // C
+            adx = shares
+            for k in range(1, nbd):
+                adx = adx + pltpu.roll(shares, bsz - k * lanes, 1)
+            adx = pltpu.roll(adx, (C - 1 - me_c) * lanes, 1) * scale
+            inside = iota((rb, bsz), 1) // lanes == C - 1 - me_c
+            adx = jnp.where(inside, adx, 0.0)
+            resid = jnp.where(inside, bs - (both - adx), 0.0)
+            adx2 = total(adx * adx)
+            res2 = total(resid * resid)
+    sums = part[0, :2, :]
     for q in range(1, R):
-        sums += part[q, :4, :]
-    dual[:4, :] = jnp.broadcast_to(jnp.sum(sums, axis=1, keepdims=True), (4, bsz))
-    dual[4:, :] = jnp.broadcast_to(omega, (4, bsz))
+        sums += part[q, :2, :]
+    dual[:2, :] = jnp.broadcast_to(jnp.sum(sums, axis=1, keepdims=True), (2, bsz))
+    dual[2:, :] = jnp.broadcast_to(omega, (6, bsz))
     for s, slot in enumerate(slots):
         q = origins(me_r, s)
         part[q] = backward(nbd, rb, cb, q, slot, codes, w_ref, wr)
@@ -238,10 +266,13 @@
     us = upper / scale
     xn = x_new[...]
     dx = xn - x_prev
-    lane = iota((1, bsz), 1)
-    out = jnp.zeros((1, bsz), F32)
-    for i, term in enumerate((dx * dx, cs * xn, us * jnp.maximum(-reduced, 0.0))):
-        out = jnp.where(lane == i, jnp.sum(term), out)
+    terms = [total(dx * dx), total(cs * xn), total(us * jnp.maximum(-reduced, 0.0)), adx2, res2]
+    sub, lane = iota((8, bsz), 0), iota((8, bsz), 1)
+    stack = jnp.zeros((8, bsz), F32)
+    for i, term in enumerate(terms):
+        stack = jnp.where(sub == i, term, stack)
+    sums = jnp.sum(stack, axis=1, keepdims=True)
+    out = total(jnp.where(sub == lane, sums, 0.0))
     p4[...] = jnp.broadcast_to(out[None], p4.shape)
 
 
@@ -253,17 +284,21 @@
     for copy in outs:
         copy.start()
     bsz = g4.shape[2]
-    primal = g4[0]
+    sums = g4[0]
     for c in range(1, C):
-        primal += g4[c]
-    lane = iota((1, bsz), 1)
-
-    def pick(i):
-        return jnp.sum(jnp.where(lane == i, primal, 0.0), axis=1, keepdims=True)
-
-    dx2, cx, uneg = (jnp.broadcast_to(pick(i), (1, bsz)) for i in range(3))
-    dy2, adx2, res2, by = (dual[i : i + 1, :] for i in range(4))
-    omega = dual[4:5, :]
+        sums += g4[c]
+    every = sums
+    for d in range(C, g4.shape[0]):
+        every += g4[d]
+    sub, lane = iota((8, bsz), 0), iota((8, bsz), 1)
+    stack = jnp.where(lane < 3, sums, every)
+    stack = jnp.broadcast_to(
+        jnp.sum(jnp.where(sub == lane, stack, 0.0), axis=1, keepdims=True), (8, bsz)
+    )
+    dx2, cx, uneg, adx2, res2 = (stack[i : i + 1, :] for i in range(5))
+    dy2, by = (dual[i : i + 1, :] for i in range(2))
+    lane = lane[:1]
+    omega = dual[2:3, :]
     movement = 0.5 * omega * dx2 + 0.5 / omega * dy2
     first = jnp.sqrt(res2 / total_rows)
     second = (cx - by + uneg) / total_cols
@@ -281,7 +316,7 @@
     nbd, bsz = blocks.shape[2], blocks.shape[3]
     rb = y_prev.shape[0] // bsz
     cb = x_prev.shape[0] // bsz
-    half = max(R // 2, 1)
+    half = min(R, 2)
     shape = lambda *dims: jax.ShapeDtypeStruct(dims, F32)
     params = pltpu.CompilerParams(vmem_limit_bytes=LIMIT)
     raw = (
@@ -317,18 +352,22 @@
     def spread(v):
         return lax.all_to_all(v, ("row", "col"), 0, 0, tiled=True)
 
-    step = R // 2
-    ids, slots = [0], [bulk]
+    def swap(v, step):
+        return lax.ppermute(v, "row", [(i, i ^ step) for i in range(R)])
+
+    far, far_ids, step = [bulk], [0], R // 2
     while step > 1:
-        slots += [lax.ppermute(b, "row", [(i, i ^ step) for i in range(R)]) for b in slots]
-        ids += [i ^ step for i in ids]
+        far += [swap(v, step) for v in far]
+        far_ids += [i ^ step for i in far_ids]
         step //= 2
+    slots, ids = far[:1], [0]
+    if R > 1:
+        slots.append(swap(bulk, 1))
+        ids.append(1)
     g1 = spread(p1)
-    g1, bulk, *slots = lax.optimization_barrier((g1, bulk, *slots[1:]))
-    slots = [bulk, *slots]
-    if R > 1:
-        slots += [lax.ppermute(b, "row", [(i, i ^ 1) for i in range(R)]) for b in slots]
-        ids += [i ^ 1 for i in ids]
+    g1, slots[-1], *far = lax.optimization_barrier((g1, slots[-1], *far[1:]))
+    slots += far + [swap(v, 1) for v in far]
+    ids += far_ids[1:] + [i ^ 1 for i in far_ids[1:]]
 
     def origins(me, s):
         return me ^ ids[s] if ids[s] else me
@@ -339,23 +378,24 @@
     ]
     part = pltpu.VMEM((R, up(cb, 8), bsz), F32)
     sizes = (nbd, R, C, rb, cb, origins)
-    dr, codes, done, colmax = pl.pallas_call(
+    dr, codes, packed, done, colmax = pl.pallas_call(
         functools.partial(scales_kernel, *sizes),
         out_shape=(
             shape(R * rb, bsz),
             shape(R, 2 * nbd, C, bsz),
+            shape(C, bsz),
             shape(R, cb, bsz),
             shape(cb, bsz),
         ),
         in_specs=[VMEM] * (1 + half),
-        out_specs=(VMEM,) * 4,
+        out_specs=(VMEM,) * 5,
         scratch_shapes=scratch,
         compiler_params=params,
         name="scales",
     )(g1, *slots[:half])
     x_new, dc, p3 = pl.pallas_call(
         functools.partial(primal_kernel, *sizes),
-        out_shape=(shape(cb, bsz), shape(cb, bsz), shape(ndev, up(2 * nbd, 8), bsz)),
+        out_shape=(shape(cb, bsz), shape(cb, bsz), shape(ndev, 1, (nbd + 1) * bsz)),
         in_specs=[VMEM] * (R - half + 6),
         out_specs=(VMEM,) * 3,
         scratch_shapes=scratch + [part],
@@ -366,12 +406,12 @@
     y_new, p4, dual = pl.pallas_call(
         functools.partial(dual_kernel, *sizes),
         out_shape=(shape(rb, bsz), shape(ndev, 1, bsz), shape(8, bsz)),
-        in_specs=[VMEM] * (R + 6),
+        in_specs=[VMEM] * (R + 7),
         out_specs=(VMEM,) * 3,
         scratch_shapes=scratch + [part],
         compiler_params=params,
         name="dual",
-    )(g3, *slots, aux, dr, codes, x_new, dc)
+    )(g3, *slots, aux, dr, codes, packed, x_new, dc)
     g4 = spread(p4)
     stats, x_new, y_new = pl.pallas_call(
         functools.partial(

time: 41.8 us -> 40.7 us (0.974)
  blocking collectives: 30.9 us -> 30.2 us
    all_to_all x3, blocking collectives: 30.9 us -> 30.2 us  [spread(): return lax.all_to_all(v, ('row', 'col'), 0, 0, tiled=True)]
  transfers between devices with their start and end apart: 3 -> 3, of which waited for: 2 -> 1; matrix products, arithmetic and copies ran while one was open for 0% -> 0% of each run, Pallas kernels for 2% -> 2%
where the time goes in v4:
time: 40.7 us; the launch traced here: 40.5 us
  blocking collectives  30.2 us (74%)
  Pallas kernels  5.17 us (13%)
  starting transfers between devices  3.12 us (8%)
  between operations  1.31 us (3%)
  waiting for transfers between devices  0.64 us (2%)
    all_to_all x3, blocking collectives, spread(): return lax.all_to_all(v, ('row', 'col'), 0, 0, tiled=True)  30.2 us
    ppermute x3, starting transfers between devices, swap(): return lax.ppermute(v, 'row', [(i, i ^ step) for i in range(R)])  3.12 us
    pallas_call x1, Pallas kernels, shards(): pl.pallas_call(functools.partial(peaks_kernel, nbd), out_shape=(shape(nde...  1.44 us
    pallas_call x1, Pallas kernels, shards(): pl.pallas_call(functools.partial(stats_kernel, C, float(y_prev.shape[0] *...  1.15 us
    pallas_call x1, Pallas kernels, shards(): pl.pallas_call(functools.partial(dual_kernel, *sizes), out_shape=(shape(r...  0.92 us
    pallas_call x1, Pallas kernels, shards(): pl.pallas_call(functools.partial(primal_kernel, *sizes), out_shape=(shape...  0.84 us
    pallas_call x1, Pallas kernels, shards(): pl.pallas_call(functools.partial(scales_kernel, *sizes), out_shape=(shape...  0.82 us
  transfers between devices with their start and end apart: 3, of which 1 were waited for; matrix products, arithmetic and copies ran while one was open for 0% of the time, Pallas kernels for 2%

profile of v4, /device:TPU:0, one launch (start us, length us, event | category | flops | bytes accessed | tf_op | source)
XLA Modules:
  0.0 40.5 jit_solution(3699477127766583914)
XLA Ops:
  1.3 1.4 %peaks.1 = (f32[32,1,640]{2,1,0:T(1,128)S(1)}, f32[576,128]{1,0:T(8,128)S(1)}, f32[32,128]{1,0:T(8,128)S(1)}) custom-call(f32[4,128,128]{2,1,0:T(8,128)} %bitcast.9, f32[32,128]{1,0:T(8,128)} %bitcast.10, f32[32,128]{1,0:T(8,128)} %bitcast.11, f32[8,128]{1,0:T(8,128)} %bitcast.12, f32[8,128]{1,0:T(8,128)} %bitcast.13, f32[8,128]{1,0:T(8,128)} %bitcast.14, ...), custom_call_target="tpu_custom_call" | custom-call | tf_op jit(solution)/shard_map/peaks/pallas_call | solution.py:333
  2.7 3.0 %collective-permute-start.1 = (f32[576,128]{1,0:T(8,128)S(1)}, f32[576,128]{1,0:T(8,128)S(1)}, u32[]{:S(2)}, u32[]{:S(2)}) collective-permute-start(f32[576,128]{1,0:T(8,128)S(1)} %get-tuple-element.24.refs_0_.refs_2_), channel_id=1, source_target_pairs={{0,16},{8,24},{16,0},{24,8},{1,17},{9,25},{17,1},{25,9},{2,18},{10... | collective-permute-start | bytes 884744 | tf_op jit(solution)/shard_map/ppermute | solution.py:356
  5.7 0.0 collective-permute-start
  5.7 12.3 %all_to_all.15.g1 = f32[32,1,640]{2,1,0:T(1,128)S(1)} all-to-all(f32[32,1,640]{2,1,0:T(1,128)S(1)} %get-tuple-element.23), channel_id=1, replica_groups=mesh['row'=4,'col'=8] {'row','col'}, dimensions={0} | all-to-all | bytes 163840 | tf_op jit(solution)/shard_map/all_to_all | solution.py:353
  18.0 0.0 collective-permute-done.1.refs_0_.refs_2_
  18.0 0.0 collective-permute-done.refs_1_
  18.0 0.1 collective-permute-start.2
  18.1 0.8 %scales.1 = (f32[128,128]{1,0:T(8,128)S(1)}, f32[4,8,8,128]{3,2,1,0:T(8,128)S(1)}, f32[8,128]{1,0:T(8,128)S(1)}, f32[4,8,128]{2,1,0:T(8,128)S(1)}, f32[8,128]{1,0:T(8,128)S(1)}) custom-call(f32[32,1,640]{2,1,0:T(1,128)S(1)} %all_to_all.15.g1, f32[576,128]{1,0:T(8,128)S(1)} %get-tuple-element.24.refs_0_.refs_2_, f32[576,128]{1,0:T(8,128)S(1)} %collective-permute-done.refs_1_), custom_call_target="tpu_custom_call" | custom-call | tf_op jit(solution)/shard_map/scales/pallas_call | solution.py:381
  19.0 0.6 %collective-permute-done.2.refs_1_.refs_3_ = f32[576,128]{1,0:T(8,128)S(1)} collective-permute-done((f32[576,128]{1,0:T(8,128)S(1)}, f32[576,128]{1,0:T(8,128)S(1)}, u32[]{:S(2)}, u32[]{:S(2)}) %collective-permute-start.2) | collective-permute-done | bytes 294944 | tf_op jit(solution)/shard_map/ppermute | solution.py:356
  19.6 0.8 %primal.1 = (f32[8,128]{1,0:T(8,128)S(1)}, f32[8,128]{1,0:T(8,128)S(1)}, f32[32,1,640]{2,1,0:T(1,128)S(1)}) custom-call(f32[576,128]{1,0:T(8,128)S(1)} %collective-permute-done.1.refs_0_.refs_2_, f32[576,128]{1,0:T(8,128)S(1)} %collective-permute-done.2.refs_1_.refs_3_, f32[576,128]{1,0:T(8,128)S(1)} %get-tuple-element.24.refs_0_.refs_2_, ...), custom_call_target="tpu_custom_call" | custom-call | tf_op jit(solution)/shard_map/primal/pallas_call | solution.py:396
  20.4 9.1 %all_to_all.16.g3 = f32[32,1,640]{2,1,0:T(1,128)S(1)} all-to-all(f32[32,1,640]{2,1,0:T(1,128)S(1)} %get-tuple-element.33), channel_id=1, replica_groups=mesh['row'=4,'col'=8] {'row','col'}, dimensions={0} | all-to-all | bytes 163840 | tf_op jit(solution)/shard_map/all_to_all | solution.py:353
  29.6 0.9 %dual.1 = (f32[32,128]{1,0:T(8,128)S(1)}, f32[32,1,128]{2,1,0:T(1,128)S(1)}, f32[8,128]{1,0:T(8,128)S(1)}) custom-call(f32[32,1,640]{2,1,0:T(1,128)S(1)} %all_to_all.16.g3, f32[576,128]{1,0:T(8,128)S(1)} %get-tuple-element.24.refs_0_.refs_2_, f32[576,128]{1,0:T(8,128)S(1)} %collective-permute-done.refs_1_, ...), custom_call_target="tpu_custom_call" | custom-call | tf_op jit(solution)/shard_map/dual/pallas_call | solution.py:406
  30.5 8.8 %all_to_all.17.g4 = f32[32,1,128]{2,1,0:T(1,128)S(1)} all-to-all(f32[32,1,128]{2,1,0:T(1,128)S(1)} %get-tuple-element.37), channel_id=1, replica_groups=mesh['row'=4,'col'=8] {'row','col'}, dimensions={0} | all-to-all | bytes 32768 | tf_op jit(solution)/shard_map/all_to_all | solution.py:353
  39.3 1.1 %stats.1 = (f32[1,3]{1,0:T(1,128)}, f32[8,128]{1,0:T(8,128)}, f32[32,128]{1,0:T(8,128)}) custom-call(f32[32,1,128]{2,1,0:T(1,128)S(1)} %all_to_all.17.g4, f32[8,128]{1,0:T(8,128)S(1)} %get-tuple-element.38.dual, f32[8,128]{1,0:T(8,128)S(1)} %get-tuple-element.35.refs_8_.x_new, f32[32,128]{1,0:T(8,128)S(1)} %get-tuple-element.39.y_new), custom_call_target="tpu_custom_call" | custom-call | tf_op jit(solution)/shard_map/stats/pallas_call | solution.py:416
Async XLA Ops:
  2.7 15.3 %collective-permute-start.1 = (f32[576,128]{1,0:T(8,128)S(1)}, f32[576,128]{1,0:T(8,128)S(1)}, u32[]{:S(2)}, u32[]{:S(2)}) collective-permute-start(f32[576,128]{1,0:T(8,128)S(1)} %get-tuple-element.24.refs_0_.refs_2_), channel_id=1, source_target_pairs={{0,16},{8,24},{16,0},{24,8},{1,17},{9,25},{17,1},{25,9},{2,18},{10... | collective-permute-start | bytes 884744 | tf_op jit(solution)/shard_map/ppermute | solution.py:356
  5.7 12.3 %collective-permute-start = (f32[576,128]{1,0:T(8,128)S(1)}, f32[576,128]{1,0:T(8,128)S(1)}, u32[]{:S(2)}, u32[]{:S(2)}) collective-permute-start(f32[576,128]{1,0:T(8,128)S(1)} %get-tuple-element.24.refs_0_.refs_2_), channel_id=1, source_target_pairs={{0,8},{8,0},{16,24},{24,16},{1,9},{9,1},{17,25},{25,17},{2,10},{10... | collective-permute-start | bytes 884744 | tf_op jit(solution)/shard_map/ppermute | solution.py:356
  18.0 1.6 %collective-permute-start.2 = (f32[576,128]{1,0:T(8,128)S(1)}, f32[576,128]{1,0:T(8,128)S(1)}, u32[]{:S(2)}, u32[]{:S(2)}) collective-permute-start(f32[576,128]{1,0:T(8,128)S(1)} %collective-permute-done.1.refs_0_.refs_2_), channel_id=1, source_target_pairs={{0,8},{8,0},{16,24},{24,16},{1,9},{9,1},{17,25},{25,17},{2,10},{10... | collective-permute-start | bytes 884744 | tf_op jit(solution)/shard_map/ppermute | solution.py:356

commit v5 on v4

--- a/solution.py
+++ b/solution.py
@@ -78,16 +78,22 @@
     aux[3 * cb :, :] = jnp.where(asub == 0, s_steps[0], s_steps[1])
 
 
-def backward(nbd, rb, cb, q, slot, codes, w_ref, wr):
+def weights(nbd, rb, groups, codes, w_ref, wr):
+    me_c = lax.axis_index("col")
+    bsz = wr.shape[1]
+    rio = iota((rb, bsz), 0).astype(F32)
+    for s, q in enumerate(groups):
+        w = w_ref[pl.ds(pl.multiple_of(q * rb, rb), rb), :]
+        for k in range(nbd):
+            hit = rio == codes[q, k, pl.ds(me_c, 1), :]
+            wr[s * nbd + k : s * nbd + k + 1, :] = total(jnp.where(hit, w, 0.0))
+    return wr[...].T
+
+
+def backward(nbd, cb, q, slot, codes, wt):
     me_c = lax.axis_index("col")
     bsz = slot.shape[1]
-    rio = iota((rb, bsz), 0).astype(F32)
     cio = iota((cb, bsz), 0).astype(F32)
-    w = w_ref[pl.ds(pl.multiple_of(q * rb, rb), rb), :]
-    for k in range(nbd):
-        hit = rio == codes[q, k, pl.ds(me_c, 1), :]
-        wr[k : k + 1, :] = total(jnp.where(hit, w, 0.0))
-    wt = wr[...].T
     out = jnp.zeros((cb, bsz), F32)
     for k in range(nbd):
         prod = total(slot[k * bsz : (k + 1) * bsz, :] * wt[:, k : k + 1])
@@ -109,7 +115,7 @@
 
 
 def scales_kernel(nbd, R, C, rb, cb, origins, g1, *refs):
-    half = min(R, 2)
+    half = R // 2 + 1 if R > 1 else 1
     slots = refs[:half]
     dr, codes, packed, part, colmax, w_ref, wr = refs[half:]
     me_r = lax.axis_index("row")
@@ -136,17 +142,19 @@
         mine = jnp.where(share == k, codes[me_r, k], mine)
     packed[...] = mine
     top = jnp.zeros((cb, bsz), F32)
-    for s, slot in enumerate(slots):
-        q = origins(me_r, s)
+    groups = [origins(me_r, s) for s in range(half)]
+    for q, slot in zip(groups, slots):
         at = pl.ds(pl.multiple_of(q * rb, rb), rb)
         w_ref[at, :] = dr[at, :] * slot[base : base + rb, :]
         top = jnp.maximum(top, col_peaks(nbd, cb, q, slot, codes))
-        part[q] = backward(nbd, rb, cb, q, slot, codes, w_ref, wr)
     colmax[...] = top
+    wt = weights(nbd, rb, groups, codes, w_ref, wr)
+    for s, (q, slot) in enumerate(zip(groups, slots)):
+        part[q] = backward(nbd, cb, q, slot, codes, wt[:, s * nbd : (s + 1) * nbd])
 
 
 def primal_kernel(nbd, R, C, rb, cb, origins, *refs):
-    half = min(R, 2)
+    half = R // 2 + 1 if R > 1 else 1
     slots, own = refs[: R - half], refs[R - half]
     aux, dr, codes, done, colmax, x_new, dc, p3, w_ref, wr, part = refs[R - half + 1 :]
     me_r = lax.axis_index("row")
@@ -161,12 +169,14 @@
     for s in range(half):
         q = origins(me_r, s)
         part[q] = done[q]
-    for s, slot in enumerate(slots):
-        q = origins(me_r, half + s)
+    groups = [origins(me_r, s) for s in range(half, R)]
+    for q, slot in zip(groups, slots):
         at = pl.ds(pl.multiple_of(q * rb, rb), rb)
         w_ref[at, :] = dr[at, :] * slot[base : base + rb, :]
         top = jnp.maximum(top, col_peaks(nbd, cb, q, slot, codes))
-        part[q] = backward(nbd, rb, cb, q, slot, codes, w_ref, wr)
+    wt = weights(nbd, rb, groups, codes, w_ref, wr)
+    for s, (q, slot) in enumerate(zip(groups, slots)):
+        part[q] = backward(nbd, cb, q, slot, codes, wt[:, s * nbd : (s + 1) * nbd])
     got = part[0]
     for q in range(1, R):
         got += part[q]
@@ -254,9 +264,10 @@
         sums += part[q, :2, :]
     dual[:2, :] = jnp.broadcast_to(jnp.sum(sums, axis=1, keepdims=True), (2, bsz))
     dual[2:, :] = jnp.broadcast_to(omega, (6, bsz))
-    for s, slot in enumerate(slots):
-        q = origins(me_r, s)
-        part[q] = backward(nbd, rb, cb, q, slot, codes, w_ref, wr)
+    groups = [origins(me_r, s) for s in range(R)]
+    wt = weights(nbd, rb, groups, codes, w_ref, wr)
+    for s, (q, slot) in enumerate(zip(groups, slots)):
+        part[q] = backward(nbd, cb, q, slot, codes, wt[:, s * nbd : (s + 1) * nbd])
     got = part[0]
     for q in range(1, R):
         got += part[q]
@@ -276,13 +287,13 @@
     p4[...] = jnp.broadcast_to(out[None], p4.shape)
 
 
-def stats_kernel(C, total_rows, total_cols, g4, dual, x_new, y_new, stats, x_out, y_out, sems):
+def stats_kernel(C, total_rows, total_cols, g4, dual, x_new, y_new, stats, x_out, y_out, last, sems):
     outs = [
-        pltpu.make_async_copy(x_new, x_out, sems.at[0]),
-        pltpu.make_async_copy(y_new, y_out, sems.at[1]),
+        pltpu.make_async_copy(a, b, sems.at[i])
+        for i, (a, b) in enumerate(((x_new, x_out), (y_new, y_out), (last, stats)))
     ]
-    for copy in outs:
-        copy.start()
+    outs[0].start()
+    outs[1].start()
     bsz = g4.shape[2]
     sums = g4[0]
     for c in range(1, C):
@@ -304,7 +315,8 @@
     second = (cx - by + uneg) / total_cols
     third = movement / jnp.sqrt(adx2 * dy2 + 1e-06)
     out = jnp.where(lane == 0, first, jnp.where(lane == 1, second, third))
-    stats[...] = out[:, : stats.shape[1]]
+    last[...] = out[:, : last.shape[1]]
+    outs[2].start()
     for copy in outs:
         copy.wait()
 
@@ -316,7 +328,8 @@
     nbd, bsz = blocks.shape[2], blocks.shape[3]
     rb = y_prev.shape[0] // bsz
     cb = x_prev.shape[0] // bsz
-    half = min(R, 2)
+    half = R // 2 + 1 if R > 1 else 1
+    in_hbm = functools.partial(pltpu.with_memory_space_constraint, memory_space=pltpu.HBM)
     shape = lambda *dims: jax.ShapeDtypeStruct(dims, F32)
     params = pltpu.CompilerParams(vmem_limit_bytes=LIMIT)
     raw = (
@@ -347,7 +360,7 @@
         ],
         compiler_params=params,
         name="peaks",
-    )(*(pltpu.with_memory_space_constraint(v, pltpu.HBM) for v in raw), counts)
+    )(*map(in_hbm, raw), counts)
 
     def spread(v):
         return lax.all_to_all(v, ("row", "col"), 0, 0, tiled=True)
@@ -374,7 +387,7 @@
 
     scratch = [
         pltpu.VMEM((R * rb, bsz), F32),
-        pltpu.VMEM((up(nbd, bsz), bsz), F32),
+        pltpu.VMEM((up(R * nbd, bsz), bsz), F32),
     ]
     part = pltpu.VMEM((R, up(cb, 8), bsz), F32)
     sizes = (nbd, R, C, rb, cb, origins)
@@ -419,8 +432,8 @@
         ),
         out_shape=(shape(1, 3), shape(cb, bsz), shape(rb, bsz)),
         in_specs=[VMEM] * 4,
-        out_specs=(VMEM, HBM, HBM),
-        scratch_shapes=[pltpu.SemaphoreType.DMA((2,))],
+        out_specs=(HBM,) * 3,
+        scratch_shapes=[pltpu.VMEM((1, 3), F32), pltpu.SemaphoreType.DMA((3,))],
         compiler_params=params,
         name="stats",
     )(g4, dual, x_new, y_new)

time: 40.7 us -> 40 us (0.983)
  Pallas kernels: 5.17 us -> 4.62 us
    pallas_call x1, Pallas kernels: 1.15 us -> 0.67 us  [shards(): pl.pallas_call(functools.partial(stats_kernel, C, float(y_prev.shape[0] *...]
where the time goes in v5:
time: 40 us; the launch traced here: 39.8 us
  blocking collectives  30.2 us (76%)
  Pallas kernels  4.62 us (12%)
  starting transfers between devices  3.12 us (8%)
  between operations  1.31 us (3%)
  waiting for transfers between devices  0.55 us (1%)
    all_to_all x3, blocking collectives, spread(): return lax.all_to_all(v, ('row', 'col'), 0, 0, tiled=True)  30.2 us
    ppermute x3, starting transfers between devices, swap(): return lax.ppermute(v, 'row', [(i, i ^ step) for i in range(R)])  3.12 us
    pallas_call x1, Pallas kernels, shards(): pl.pallas_call(functools.partial(peaks_kernel, nbd), out_shape=(shape(nde...  1.44 us
    pallas_call x1, Pallas kernels, shards(): pl.pallas_call(functools.partial(scales_kernel, *sizes), out_shape=(shape...  0.92 us
    pallas_call x1, Pallas kernels, shards(): pl.pallas_call(functools.partial(dual_kernel, *sizes), out_shape=(shape(r...  0.88 us
  transfers between devices with their start and end apart: 3, of which 1 were waited for; matrix products, arithmetic and copies ran while one was open for 0% of the time, Pallas kernels for 2%

profile of v5, /device:TPU:0, one launch (start us, length us, event | category | flops | bytes accessed | tf_op | source)
XLA Modules:
  0.0 39.8 jit_solution(2954839472239118850)
XLA Ops:
  1.3 1.4 %peaks.1 = (f32[32,1,640]{2,1,0:T(1,128)S(1)}, f32[576,128]{1,0:T(8,128)S(1)}, f32[32,128]{1,0:T(8,128)S(1)}) custom-call(f32[4,128,128]{2,1,0:T(8,128)} %bitcast.9, f32[32,128]{1,0:T(8,128)} %bitcast.10, f32[32,128]{1,0:T(8,128)} %bitcast.11, f32[8,128]{1,0:T(8,128)} %bitcast.12, f32[8,128]{1,0:T(8,128)} %bitcast.13, f32[8,128]{1,0:T(8,128)} %bitcast.14, ...), custom_call_target="tpu_custom_call" | custom-call | tf_op jit(solution)/shard_map/peaks/pallas_call | solution.py:346
  2.7 3.0 %collective-permute-start.1 = (f32[576,128]{1,0:T(8,128)S(1)}, f32[576,128]{1,0:T(8,128)S(1)}, u32[]{:S(2)}, u32[]{:S(2)}) collective-permute-start(f32[576,128]{1,0:T(8,128)S(1)} %get-tuple-element.24.refs_0_.refs_1_), channel_id=1, source_target_pairs={{0,16},{8,24},{16,0},{24,8},{1,17},{9,25},{17,1},{25,9},{2,18},{10... | collective-permute-start | bytes 884744 | tf_op jit(solution)/shard_map/ppermute | solution.py:369
  5.7 0.0 collective-permute-start
  5.7 12.3 %all_to_all.15.g1 = f32[32,1,640]{2,1,0:T(1,128)S(1)} all-to-all(f32[32,1,640]{2,1,0:T(1,128)S(1)} %get-tuple-element.23), channel_id=1, replica_groups=mesh['row'=4,'col'=8] {'row','col'}, dimensions={0} | all-to-all | bytes 163840 | tf_op jit(solution)/shard_map/all_to_all | solution.py:366
  18.0 0.0 collective-permute-done.1.refs_2_
  18.0 0.0 collective-permute-done.refs_1_
  18.0 0.1 collective-permute-start.2
  18.1 0.9 %scales.1 = (f32[128,128]{1,0:T(8,128)S(1)}, f32[4,8,8,128]{3,2,1,0:T(8,128)S(1)}, f32[8,128]{1,0:T(8,128)S(1)}, f32[4,8,128]{2,1,0:T(8,128)S(1)}, f32[8,128]{1,0:T(8,128)S(1)}) custom-call(f32[32,1,640]{2,1,0:T(1,128)S(1)} %all_to_all.15.g1, f32[576,128]{1,0:T(8,128)S(1)} %get-tuple-element.24.refs_0_.refs_1_, f32[576,128]{1,0:T(8,128)S(1)} %collective-permute-done.refs_1_, ...), custom_call_target="tpu_custom_call" | custom-call | tf_op jit(solution)/shard_map/scales/pallas_call | solution.py:394
  19.1 0.5 %collective-permute-done.2.refs_0_.refs_3_ = f32[576,128]{1,0:T(8,128)S(1)} collective-permute-done((f32[576,128]{1,0:T(8,128)S(1)}, f32[576,128]{1,0:T(8,128)S(1)}, u32[]{:S(2)}, u32[]{:S(2)}) %collective-permute-start.2) | collective-permute-done | bytes 294944 | tf_op jit(solution)/shard_map/ppermute | solution.py:369
  19.6 0.7 %primal.1 = (f32[8,128]{1,0:T(8,128)S(1)}, f32[8,128]{1,0:T(8,128)S(1)}, f32[32,1,640]{2,1,0:T(1,128)S(1)}) custom-call(f32[576,128]{1,0:T(8,128)S(1)} %collective-permute-done.2.refs_0_.refs_3_, f32[576,128]{1,0:T(8,128)S(1)} %get-tuple-element.24.refs_0_.refs_1_, f32[32,128]{1,0:T(8,128)S(1)} %get-tuple-element.26.refs_2_.refs_4_, ...), custom_call_target="tpu_custom_call" | custom-call | tf_op jit(solution)/shard_map/primal/pallas_call | solution.py:409
  20.3 9.1 %all_to_all.16.g3 = f32[32,1,640]{2,1,0:T(1,128)S(1)} all-to-all(f32[32,1,640]{2,1,0:T(1,128)S(1)} %get-tuple-element.33), channel_id=1, replica_groups=mesh['row'=4,'col'=8] {'row','col'}, dimensions={0} | all-to-all | bytes 163840 | tf_op jit(solution)/shard_map/all_to_all | solution.py:366
  29.5 0.9 %dual.1 = (f32[32,128]{1,0:T(8,128)S(1)}, f32[32,1,128]{2,1,0:T(1,128)S(1)}, f32[8,128]{1,0:T(8,128)S(1)}) custom-call(f32[32,1,640]{2,1,0:T(1,128)S(1)} %all_to_all.16.g3, f32[576,128]{1,0:T(8,128)S(1)} %get-tuple-element.24.refs_0_.refs_1_, f32[576,128]{1,0:T(8,128)S(1)} %collective-permute-done.refs_1_, f32[576,128]{1,0:T(8,128)S(1)} %collective-permute-done.1.refs_2_, ...), custom_call_target="tpu_custom_call" | custom-call | tf_op jit(solution)/shard_map/dual/pallas_call | solution.py:419
  30.3 8.8 %all_to_all.17.g4 = f32[32,1,128]{2,1,0:T(1,128)S(1)} all-to-all(f32[32,1,128]{2,1,0:T(1,128)S(1)} %get-tuple-element.37), channel_id=1, replica_groups=mesh['row'=4,'col'=8] {'row','col'}, dimensions={0} | all-to-all | bytes 32768 | tf_op jit(solution)/shard_map/all_to_all | solution.py:366
  39.2 0.7 %stats.1 = (f32[1,3]{1,0:T(1,128)}, f32[8,128]{1,0:T(8,128)}, f32[32,128]{1,0:T(8,128)}) custom-call(f32[32,1,128]{2,1,0:T(1,128)S(1)} %all_to_all.17.g4, f32[8,128]{1,0:T(8,128)S(1)} %get-tuple-element.38.dual, f32[8,128]{1,0:T(8,128)S(1)} %get-tuple-element.35.refs_8_.x_new, f32[32,128]{1,0:T(8,128)S(1)} %get-tuple-element.39.y_new), custom_call_target="tpu_custom_call" | custom-call | tf_op jit(solution)/shard_map/stats/pallas_call | solution.py:429
Async XLA Ops:
  2.7 15.3 %collective-permute-start.1 = (f32[576,128]{1,0:T(8,128)S(1)}, f32[576,128]{1,0:T(8,128)S(1)}, u32[]{:S(2)}, u32[]{:S(2)}) collective-permute-start(f32[576,128]{1,0:T(8,128)S(1)} %get-tuple-element.24.refs_0_.refs_1_), channel_id=1, source_target_pairs={{0,16},{8,24},{16,0},{24,8},{1,17},{9,25},{17,1},{25,9},{2,18},{10... | collective-permute-start | bytes 884744 | tf_op jit(solution)/shard_map/ppermute | solution.py:369
  5.7 12.3 %collective-permute-start = (f32[576,128]{1,0:T(8,128)S(1)}, f32[576,128]{1,0:T(8,128)S(1)}, u32[]{:S(2)}, u32[]{:S(2)}) collective-permute-start(f32[576,128]{1,0:T(8,128)S(1)} %get-tuple-element.24.refs_0_.refs_1_), channel_id=1, source_target_pairs={{0,8},{8,0},{16,24},{24,16},{1,9},{9,1},{17,25},{25,17},{2,10},{10... | collective-permute-start | bytes 884744 | tf_op jit(solution)/shard_map/ppermute | solution.py:369
  18.0 1.6 %collective-permute-start.2 = (f32[576,128]{1,0:T(8,128)S(1)}, f32[576,128]{1,0:T(8,128)S(1)}, u32[]{:S(2)}, u32[]{:S(2)}) collective-permute-start(f32[576,128]{1,0:T(8,128)S(1)} %collective-permute-done.1.refs_2_), channel_id=1, source_target_pairs={{0,8},{8,0},{16,24},{24,16},{1,9},{9,1},{17,25},{25,17},{2,10},{10... | collective-permute-start | bytes 884744 | tf_op jit(solution)/shard_map/ppermute | solution.py:369

commit v6 on v5

--- a/solution.py
+++ b/solution.py
@@ -12,6 +12,7 @@
 SMEM = pl.BlockSpec(memory_space=pltpu.SMEM)
 HBM = pl.BlockSpec(memory_space=pltpu.HBM)
 LIMIT = 40 * 1024 * 1024
+SPLITS = 3
 
 
 def up(n, m):
@@ -22,25 +23,18 @@
     return lax.broadcasted_iota(jnp.int32, shape, dim)
 
 
-def rows_of(vectors, bsz):
-    lane = iota((bsz, bsz), 1)
-    cols = jnp.zeros((bsz, bsz), F32)
-    for k, col in enumerate(vectors):
-        cols = jnp.where(lane == k, col, cols)
-    return cols.T
-
-
 def total(rows):
     return jnp.sum(rows, axis=0, keepdims=True)
 
 
-def peaks_kernel(nbd, blocks, y, rhs, x, cost, upper, brow, bcol, steps, count, p1, bulk, aux, *scratch):
+def peaks_kernel(nbd, blocks, y, rhs, x, cost, upper, brow, bcol, steps, count, p1, bulk, aux, turned, *scratch):
     s_row, s_col, s_steps, sems = scratch
     bsz = bulk.shape[1]
     rb = y.shape[0]
     cb = x.shape[0]
     base = nbd * bsz
     pairs = [
+        (blocks, bulk.at[:base]),
         (brow, s_row),
         (bcol, s_col),
         (steps, s_steps),
@@ -50,20 +44,17 @@
         (cost, aux.at[cb : 2 * cb]),
         (upper, aux.at[2 * cb : 3 * cb]),
     ]
-    loads = [
-        pltpu.make_async_copy(blocks.at[k], bulk.at[k * bsz : (k + 1) * bsz], sems.at[k])
-        for k in range(nbd)
-    ]
-    rest = [pltpu.make_async_copy(a, b, sems.at[nbd + i]) for i, (a, b) in enumerate(pairs)]
-    for copy in loads + rest:
+    loads = [pltpu.make_async_copy(a, b, sems.at[i]) for i, (a, b) in enumerate(pairs)]
+    for copy in loads:
         copy.start()
+    loads[0].wait()
     peaks = []
     for k in range(nbd):
-        loads[k].wait()
         a = bulk[k * bsz : (k + 1) * bsz, :]
-        peaks.append(jnp.max(jnp.abs(a), axis=1, keepdims=True))
-    rows = rows_of(peaks, bsz)
-    for copy in rest:
+        a = a.T
+        turned[k * bsz : (k + 1) * bsz, :] = a
+        peaks.append(jnp.max(jnp.abs(a), axis=0, keepdims=True))
+    for copy in loads[1:]:
         copy.wait()
     lane = iota((1, bsz), 1)
     meta = jnp.full((1, bsz), -1.0, F32)
@@ -71,34 +62,51 @@
         code = jnp.where(k < count[0, 0], s_row[0, 0, k], -1).astype(F32)
         meta = jnp.where(lane == k, code, meta)
         meta = jnp.where(lane == nbd + k, s_col[0, 0, k].astype(F32), meta)
-    pieces = [rows[k : k + 1, :] for k in range(nbd)] + [meta]
-    for k, piece in enumerate(pieces):
+    for k, piece in enumerate(peaks + [meta]):
         p1[:, :, k * bsz : (k + 1) * bsz] = jnp.broadcast_to(piece[None], (p1.shape[0], 1, bsz))
     asub = iota((8, bsz), 0)
     aux[3 * cb :, :] = jnp.where(asub == 0, s_steps[0], s_steps[1])
 
 
-def weights(nbd, rb, groups, codes, w_ref, wr):
+def split(v):
+    parts = []
+    for _ in range(SPLITS):
+        top = v.astype(jnp.bfloat16).astype(F32)
+        parts.append(top)
+        v = v - top
+    return parts
+
+
+def split_blocks(nbd, slot, out):
+    bsz = slot.shape[1]
+    for k in range(nbd):
+        at = slice(k * bsz, (k + 1) * bsz)
+        for i, v in enumerate(split(slot[at, :])):
+            out[i, at, :] = v.astype(jnp.bfloat16)
+
+
+def product(left, right, dims):
+    n = left.shape[0]
+    left = jnp.concatenate(split(left), axis=0).astype(jnp.bfloat16)
+    out = 0.0
+    for j in range(SPLITS):
+        got = lax.dot_general(left, right(j), (dims, ((), ())), preferred_element_type=F32)
+        for i in range(SPLITS - j):
+            out = out + got[i * n : (i + 1) * n]
+    return out
+
+
+def backward(nbd, rb, cb, q, parts, codes, w_ref):
     me_c = lax.axis_index("col")
-    bsz = wr.shape[1]
+    bsz = w_ref.shape[1]
     rio = iota((rb, bsz), 0).astype(F32)
-    for s, q in enumerate(groups):
-        w = w_ref[pl.ds(pl.multiple_of(q * rb, rb), rb), :]
-        for k in range(nbd):
-            hit = rio == codes[q, k, pl.ds(me_c, 1), :]
-            wr[s * nbd + k : s * nbd + k + 1, :] = total(jnp.where(hit, w, 0.0))
-    return wr[...].T
-
-
-def backward(nbd, cb, q, slot, codes, wt):
-    me_c = lax.axis_index("col")
-    bsz = slot.shape[1]
     cio = iota((cb, bsz), 0).astype(F32)
-    out = jnp.zeros((cb, bsz), F32)
-    for k in range(nbd):
-        prod = total(slot[k * bsz : (k + 1) * bsz, :] * wt[:, k : k + 1])
-        out += jnp.where(cio == codes[q, nbd + k, pl.ds(me_c, 1), :], prod, 0.0)
-    return out
+    w = w_ref[pl.ds(pl.multiple_of(q * rb, rb), rb), :]
+    picks = []
+    for k in range(nbd):
+        row = total(jnp.where(rio == codes[q, k, pl.ds(me_c, 1), :], w, 0.0))
+        picks.append(jnp.where(cio == codes[q, nbd + k, pl.ds(me_c, 1), :], row, 0.0))
+    return product(jnp.concatenate(picks, axis=1), lambda i: parts[i], ((1,), (0,)))
 
 
 def col_peaks(nbd, cb, q, slot, codes):
@@ -114,15 +122,14 @@
     return out
 
 
-def scales_kernel(nbd, R, C, rb, cb, origins, g1, *refs):
+def scales_kernel(nbd, R, C, rb, cb, origins, g1, turned, *refs):
     half = R // 2 + 1 if R > 1 else 1
     slots = refs[:half]
-    dr, codes, packed, part, colmax, w_ref, wr = refs[half:]
+    dr, codes, packed, part, colmax, parts, own, w_ref = refs[half:]
     me_r = lax.axis_index("row")
     bsz = dr.shape[1]
     base = nbd * bsz
     rio = iota((rb, bsz), 0).astype(F32)
-    wr[...] = jnp.zeros_like(wr)
     for q in range(R):
         meta = g1[q * C : (q + 1) * C, 0, base:]
         for k in range(2 * nbd):
@@ -148,15 +155,16 @@
         w_ref[at, :] = dr[at, :] * slot[base : base + rb, :]
         top = jnp.maximum(top, col_peaks(nbd, cb, q, slot, codes))
     colmax[...] = top
-    wt = weights(nbd, rb, groups, codes, w_ref, wr)
     for s, (q, slot) in enumerate(zip(groups, slots)):
-        part[q] = backward(nbd, cb, q, slot, codes, wt[:, s * nbd : (s + 1) * nbd])
+        split_blocks(nbd, slot, parts.at[s])
+        part[q] = backward(nbd, rb, cb, q, parts.at[s], codes, w_ref)
+    split_blocks(nbd, turned, own)
 
 
 def primal_kernel(nbd, R, C, rb, cb, origins, *refs):
     half = R // 2 + 1 if R > 1 else 1
     slots, own = refs[: R - half], refs[R - half]
-    aux, dr, codes, done, colmax, x_new, dc, p3, w_ref, wr, part = refs[R - half + 1 :]
+    aux, dr, codes, done, colmax, x_new, dc, p3, parts, w_ref, part = refs[R - half + 1 :]
     me_r = lax.axis_index("row")
     me_c = lax.axis_index("col")
     bsz = x_new.shape[1]
@@ -164,7 +172,6 @@
     x_prev, cost, upper = (aux[i * cb : (i + 1) * cb, :] for i in range(3))
     eta, omega = (aux[3 * cb + i : 3 * cb + i + 1, :] for i in range(2))
     cio = iota((cb, bsz), 0).astype(F32)
-    wr[...] = jnp.zeros_like(wr)
     top = colmax[...]
     for s in range(half):
         q = origins(me_r, s)
@@ -174,9 +181,9 @@
         at = pl.ds(pl.multiple_of(q * rb, rb), rb)
         w_ref[at, :] = dr[at, :] * slot[base : base + rb, :]
         top = jnp.maximum(top, col_peaks(nbd, cb, q, slot, codes))
-    wt = weights(nbd, rb, groups, codes, w_ref, wr)
     for s, (q, slot) in enumerate(zip(groups, slots)):
-        part[q] = backward(nbd, cb, q, slot, codes, wt[:, s * nbd : (s + 1) * nbd])
+        split_blocks(nbd, slot, parts.at[s])
+        part[q] = backward(nbd, rb, cb, q, parts.at[s], codes, w_ref)
     got = part[0]
     for q in range(1, R):
         got += part[q]
@@ -187,31 +194,30 @@
     x_new[...] = xn
     v2 = scale * (xn - x_prev)
     v1 = scale * xn + v2
-    both, step = [], []
-    for k in range(nbd):
-        a = own[k * bsz : (k + 1) * bsz, :]
+    sub = iota((up(2 * nbd, 8), bsz), 0)
+    picks = []
+    for k in range(nbd):
         hit = cio == codes[me_r, nbd + k, pl.ds(me_c, 1), :]
-        for v, out in ((v1, both), (v2, step)):
-            out.append(jnp.sum(a * total(jnp.where(hit, v, 0.0)), axis=1, keepdims=True))
-    rows = rows_of(both + step, bsz)
+        one, two = (total(jnp.where(hit, v, 0.0)) for v in (v1, v2))
+        picks.append(jnp.where(sub == k, one, jnp.where(sub == nbd + k, two, 0.0)))
+    rows = product(jnp.concatenate(picks, axis=1), lambda i: own[i], ((1,), (0,)))
     lanes = bsz // C
-    share = iota((C, bsz), 1) // lanes
+    turn = (iota((C, bsz), 1) // lanes + iota((C, bsz), 0)) % C
     row = jnp.zeros((C, bsz), F32)
     for k in range(nbd):
         part_k = pltpu.roll(rows[nbd + k : nbd + k + 1, :], (k + 1) * lanes % bsz, 1)
-        part_k = jnp.broadcast_to(part_k, (C, bsz))
-        part_k = pltpu.roll(part_k, 0, 1, stride=lanes, stride_axis=0)
-        row = jnp.where(share == k, part_k, row)
+        row = jnp.where(turn == k, part_k, row)
         p3[:, :, k * bsz : (k + 1) * bsz] = jnp.broadcast_to(
             rows[k : k + 1, :][None], (p3.shape[0], 1, bsz)
         )
+    row = pltpu.roll(row, 0, 1, stride=lanes, stride_axis=0)
     for q in range(R):
         p3[q * C : (q + 1) * C, 0, base:] = row
 
 
 def dual_kernel(nbd, R, C, rb, cb, origins, g3, *refs):
     slots = refs[:R]
-    aux, dr, codes, packed, x_new, dc, y_new, p4, dual, w_ref, wr, part = refs[R:]
+    early, late, aux, dr, codes, packed, x_new, dc, y_new, p4, dual, w_ref, part = refs[R:]
     me_r = lax.axis_index("row")
     me_c = lax.axis_index("col")
     bsz = x_new.shape[1]
@@ -219,7 +225,6 @@
     x_prev, cost, upper = (aux[i * cb : (i + 1) * cb, :] for i in range(3))
     eta, omega = (aux[3 * cb + i : 3 * cb + i + 1, :] for i in range(2))
     rio = iota((rb, bsz), 0).astype(F32)
-    wr[...] = jnp.zeros_like(wr)
     sigma = eta * omega
     for s, slot in enumerate(slots):
         q = origins(me_r, s)
@@ -265,9 +270,10 @@
     dual[:2, :] = jnp.broadcast_to(jnp.sum(sums, axis=1, keepdims=True), (2, bsz))
     dual[2:, :] = jnp.broadcast_to(omega, (6, bsz))
     groups = [origins(me_r, s) for s in range(R)]
-    wt = weights(nbd, rb, groups, codes, w_ref, wr)
-    for s, (q, slot) in enumerate(zip(groups, slots)):
-        part[q] = backward(nbd, cb, q, slot, codes, wt[:, s * nbd : (s + 1) * nbd])
+    half = early.shape[0]
+    for s, q in enumerate(groups):
+        parts = early.at[s] if s < half else late.at[s - half]
+        part[q] = backward(nbd, rb, cb, q, parts, codes, w_ref)
     got = part[0]
     for q in range(1, R):
         got += part[q]
@@ -333,7 +339,7 @@
     shape = lambda *dims: jax.ShapeDtypeStruct(dims, F32)
     params = pltpu.CompilerParams(vmem_limit_bytes=LIMIT)
     raw = (
-        blocks[0, 0],
+        blocks.reshape(nbd * bsz, bsz),
         y_prev.reshape(rb, bsz),
         rhs.reshape(rb, bsz),
         x_prev.reshape(cb, bsz),
@@ -343,20 +349,21 @@
         block_cols,
         steps,
     )
-    p1, bulk, aux = pl.pallas_call(
+    p1, bulk, aux, turned = pl.pallas_call(
         functools.partial(peaks_kernel, nbd),
         out_shape=(
             shape(ndev, 1, (nbd + 1) * bsz),
             shape(nbd * bsz + 2 * rb, bsz),
             shape(3 * cb + 8, bsz),
+            shape(nbd * bsz, bsz),
         ),
         in_specs=[HBM] * len(raw) + [SMEM],
-        out_specs=(VMEM,) * 3,
+        out_specs=(VMEM,) * 4,
         scratch_shapes=[
             pltpu.SMEM((1, 1, nbd), jnp.int32),
             pltpu.SMEM((1, 1, nbd), jnp.int32),
             pltpu.SMEM(steps.shape, F32),
-            pltpu.SemaphoreType.DMA((nbd + 8,)),
+            pltpu.SemaphoreType.DMA((9,)),
         ],
         compiler_params=params,
         name="peaks",
@@ -385,13 +392,14 @@
     def origins(me, s):
         return me ^ ids[s] if ids[s] else me
 
-    scratch = [
-        pltpu.VMEM((R * rb, bsz), F32),
-        pltpu.VMEM((up(R * nbd, bsz), bsz), F32),
-    ]
+    scratch = [pltpu.VMEM((R * rb, bsz), F32)]
+
+    def parts_of(n):
+        return jax.ShapeDtypeStruct((n, SPLITS, nbd * bsz, bsz), jnp.bfloat16)
+
     part = pltpu.VMEM((R, up(cb, 8), bsz), F32)
     sizes = (nbd, R, C, rb, cb, origins)
-    dr, codes, packed, done, colmax = pl.pallas_call(
+    dr, codes, packed, done, colmax, early, own = pl.pallas_call(
         functools.partial(scales_kernel, *sizes),
         out_shape=(
             shape(R * rb, bsz),
@@ -399,32 +407,39 @@
             shape(C, bsz),
             shape(R, cb, bsz),
             shape(cb, bsz),
+            parts_of(half),
+            jax.ShapeDtypeStruct((SPLITS, nbd * bsz, bsz), jnp.bfloat16),
         ),
-        in_specs=[VMEM] * (1 + half),
-        out_specs=(VMEM,) * 5,
+        in_specs=[VMEM] * (2 + half),
+        out_specs=(VMEM,) * 7,
         scratch_shapes=scratch,
         compiler_params=params,
         name="scales",
-    )(g1, *slots[:half])
-    x_new, dc, p3 = pl.pallas_call(
+    )(g1, turned, *slots[:half])
+    x_new, dc, p3, late = pl.pallas_call(
         functools.partial(primal_kernel, *sizes),
-        out_shape=(shape(cb, bsz), shape(cb, bsz), shape(ndev, 1, (nbd + 1) * bsz)),
+        out_shape=(
+            shape(cb, bsz),
+            shape(cb, bsz),
+            shape(ndev, 1, (nbd + 1) * bsz),
+            parts_of(max(R - half, 1)),
+        ),
         in_specs=[VMEM] * (R - half + 6),
-        out_specs=(VMEM,) * 3,
+        out_specs=(VMEM,) * 4,
         scratch_shapes=scratch + [part],
         compiler_params=params,
         name="primal",
-    )(*slots[half:], bulk, aux, dr, codes, done, colmax)
+    )(*slots[half:], own, aux, dr, codes, done, colmax)
     g3 = spread(p3)
     y_new, p4, dual = pl.pallas_call(
         functools.partial(dual_kernel, *sizes),
         out_shape=(shape(rb, bsz), shape(ndev, 1, bsz), shape(8, bsz)),
-        in_specs=[VMEM] * (R + 7),
+        in_specs=[VMEM] * (R + 9),
         out_specs=(VMEM,) * 3,
         scratch_shapes=scratch + [part],
         compiler_params=params,
         name="dual",
-    )(g3, *slots, aux, dr, codes, packed, x_new, dc)
+    )(g3, *slots, early, late, aux, dr, codes, packed, x_new, dc)
     g4 = spread(p4)
     stats, x_new, y_new = pl.pallas_call(
         functools.partial(

time: 40 us -> 39.5 us (0.988)
  Pallas kernels: 4.62 us -> 4.09 us
where the time goes in v6:
time: 39.5 us; the launch traced here: 39.3 us
  blocking collectives  30.2 us (76%)
  Pallas kernels  4.09 us (10%)
  starting transfers between devices  3.12 us (8%)
  between operations  1.31 us (3%)
  waiting for transfers between devices  0.58 us (1%)
    all_to_all x3, blocking collectives, spread(): return lax.all_to_all(v, ('row', 'col'), 0, 0, tiled=True)  30.2 us
    ppermute x3, starting transfers between devices, swap(): return lax.ppermute(v, 'row', [(i, i ^ step) for i in range(R)])  3.12 us
    pallas_call x1, Pallas kernels, shards(): pl.pallas_call(functools.partial(peaks_kernel, nbd), out_shape=(shape(nde...  1.25 us
    pallas_call x1, Pallas kernels, shards(): pl.pallas_call(functools.partial(scales_kernel, *sizes), out_shape=(shape...  0.89 us
  transfers between devices with their start and end apart: 3, of which 1 were waited for; matrix products, arithmetic and copies ran while one was open for 0% of the time, Pallas kernels for 2%

profile of v6, /device:TPU:0, one launch (start us, length us, event | category | flops | bytes accessed | tf_op | source)
XLA Modules:
  0.0 39.3 jit_solution(3273118402813211747)
XLA Ops:
  1.3 1.2 %peaks.1 = (f32[32,1,640]{2,1,0:T(1,128)S(1)}, f32[576,128]{1,0:T(8,128)S(1)}, f32[32,128]{1,0:T(8,128)S(1)}, f32[512,128]{1,0:T(8,128)S(1)}) custom-call(f32[512,128]{1,0:T(8,128)} %bitcast.9, f32[32,128]{1,0:T(8,128)} %bitcast.10, f32[32,128]{1,0:T(8,128)} %bitcast.11, f32[8,128]{1,0:T(8,128)} %bitcast.12, f32[8,128]{1,0:T(8,128)} %bitcast.13, ...), custom_call_target="tpu_custom_call" | custom-call | tf_op jit(solution)/shard_map/peaks/pallas_call | solution.py:352
  2.5 3.0 %collective-permute-start.1 = (f32[576,128]{1,0:T(8,128)S(1)}, f32[576,128]{1,0:T(8,128)S(1)}, u32[]{:S(2)}, u32[]{:S(2)}) collective-permute-start(f32[576,128]{1,0:T(8,128)S(1)} %get-tuple-element.28.refs_0_), channel_id=1, source_target_pairs={{0,16},{8,24},{16,0},{24,8},{1,17},{9,25},{17,1},{25,9},{2,18},{10... | collective-permute-start | bytes 884744 | tf_op jit(solution)/shard_map/ppermute | solution.py:376
  5.5 0.0 collective-permute-start
  5.5 12.3 %all_to_all.15.g1 = f32[32,1,640]{2,1,0:T(1,128)S(1)} all-to-all(f32[32,1,640]{2,1,0:T(1,128)S(1)} %get-tuple-element.27), channel_id=1, replica_groups=mesh['row'=4,'col'=8] {'row','col'}, dimensions={0} | all-to-all | bytes 163840 | tf_op jit(solution)/shard_map/all_to_all | solution.py:373
  17.8 0.0 collective-permute-done.1.refs_2_
  17.8 0.0 collective-permute-done.refs_1_
  17.8 0.1 collective-permute-start.2
  17.9 0.9 %scales.1 = (f32[128,128]{1,0:T(8,128)S(1)}, f32[4,8,8,128]{3,2,1,0:T(8,128)S(1)}, f32[8,128]{1,0:T(8,128)S(1)}, f32[4,8,128]{2,1,0:T(8,128)S(1)}, f32[8,128]{1,...) custom-call(f32[32,1,640]{2,1,0:T(1,128)S(1)} %all_to_all.15.g1, ...), custom_call_target="tpu_custom_call" | custom-call | tf_op jit(solution)/shard_map/scales/pallas_call | solution.py:402
  18.8 0.6 %collective-permute-done.2.refs_0_.refs_3_ = f32[576,128]{1,0:T(8,128)S(1)} collective-permute-done((f32[576,128]{1,0:T(8,128)S(1)}, f32[576,128]{1,0:T(8,128)S(1)}, u32[]{:S(2)}, u32[]{:S(2)}) %collective-permute-start.2) | collective-permute-done | bytes 294944 | tf_op jit(solution)/shard_map/ppermute | solution.py:376
  19.4 0.6 %primal.1 = (f32[8,128]{1,0:T(8,128)S(1)}, f32[8,128]{1,0:T(8,128)S(1)}, f32[32,1,640]{2,1,0:T(1,128)S(1)}, bf16[1,3,512,128]{3,2,1,0:T(8,128)(2,1)S(1)}) custom-call(f32[576,128]{1,0:T(8,128)S(1)} %collective-permute-done.2.refs_0_.refs_3_, bf16[3,512,128]{2,1,0:T(8,128)(2,1)S(1)} %get-tuple-element.33.refs_1_, ...), custom_call_target="tpu_custom_call" | custom-call | tf_op jit(solution)/shard_map/primal/pallas_call | solution.py:419
  20.0 9.1 %all_to_all.16.g3 = f32[32,1,640]{2,1,0:T(1,128)S(1)} all-to-all(f32[32,1,640]{2,1,0:T(1,128)S(1)} %get-tuple-element.39), channel_id=1, replica_groups=mesh['row'=4,'col'=8] {'row','col'}, dimensions={0} | all-to-all | bytes 163840 | tf_op jit(solution)/shard_map/all_to_all | solution.py:373
  29.1 0.7 %dual.1 = (f32[32,128]{1,0:T(8,128)S(1)}, f32[32,1,128]{2,1,0:T(1,128)S(1)}, f32[8,128]{1,0:T(8,128)S(1)}) custom-call(f32[32,1,640]{2,1,0:T(1,128)S(1)} %all_to_all.16.g3, f32[576,128]{1,0:T(8,128)S(1)} %get-tuple-element.28.refs_0_, f32[576,128]{1,0:T(8,128)S(1)} %collective-permute-done.refs_1_, f32[576,128]{1,0:T(8,128)S(1)} %collective-permute-done.1.refs_2_, ...), custom_call_target="tpu_custom_call" | custom-call | tf_op jit(solution)/shard_map/dual/pallas_call | solution.py:434
  29.8 8.8 %all_to_all.17.g4 = f32[32,1,128]{2,1,0:T(1,128)S(1)} all-to-all(f32[32,1,128]{2,1,0:T(1,128)S(1)} %get-tuple-element.45), channel_id=1, replica_groups=mesh['row'=4,'col'=8] {'row','col'}, dimensions={0} | all-to-all | bytes 32768 | tf_op jit(solution)/shard_map/all_to_all | solution.py:373
  38.6 0.7 %stats.1 = (f32[1,3]{1,0:T(1,128)}, f32[8,128]{1,0:T(8,128)}, f32[32,128]{1,0:T(8,128)}) custom-call(f32[32,1,128]{2,1,0:T(1,128)S(1)} %all_to_all.17.g4, f32[8,128]{1,0:T(8,128)S(1)} %get-tuple-element.46.dual, f32[8,128]{1,0:T(8,128)S(1)} %get-tuple-element.43.refs_10_.x_new, f32[32,128]{1,0:T(8,128)S(1)} %get-tuple-element.47.y_new), custom_call_target="tpu_custom_call" | custom-call | tf_op jit(solution)/shard_map/stats/pallas_call | solution.py:444
Async XLA Ops:
  2.5 15.3 %collective-permute-start.1 = (f32[576,128]{1,0:T(8,128)S(1)}, f32[576,128]{1,0:T(8,128)S(1)}, u32[]{:S(2)}, u32[]{:S(2)}) collective-permute-start(f32[576,128]{1,0:T(8,128)S(1)} %get-tuple-element.28.refs_0_), channel_id=1, source_target_pairs={{0,16},{8,24},{16,0},{24,8},{1,17},{9,25},{17,1},{25,9},{2,18},{10... | collective-permute-start | bytes 884744 | tf_op jit(solution)/shard_map/ppermute | solution.py:376
  5.5 12.3 %collective-permute-start = (f32[576,128]{1,0:T(8,128)S(1)}, f32[576,128]{1,0:T(8,128)S(1)}, u32[]{:S(2)}, u32[]{:S(2)}) collective-permute-start(f32[576,128]{1,0:T(8,128)S(1)} %get-tuple-element.28.refs_0_), channel_id=1, source_target_pairs={{0,8},{8,0},{16,24},{24,16},{1,9},{9,1},{17,25},{25,17},{2,10},{10... | collective-permute-start | bytes 884744 | tf_op jit(solution)/shard_map/ppermute | solution.py:376
  17.8 1.6 %collective-permute-start.2 = (f32[576,128]{1,0:T(8,128)S(1)}, f32[576,128]{1,0:T(8,128)S(1)}, u32[]{:S(2)}, u32[]{:S(2)}) collective-permute-start(f32[576,128]{1,0:T(8,128)S(1)} %collective-permute-done.1.refs_2_), channel_id=1, source_target_pairs={{0,8},{8,0},{16,24},{24,16},{1,9},{9,1},{17,25},{25,17},{2,10},{10... | collective-permute-start | bytes 884744 | tf_op jit(solution)/shard_map/ppermute | solution.py:376

commit v7 on v6

--- a/solution.py
+++ b/solution.py
@@ -70,8 +70,10 @@
 
 def split(v):
     parts = []
+    most = float(jnp.finfo(jnp.bfloat16).max)
     for _ in range(SPLITS):
-        top = v.astype(jnp.bfloat16).astype(F32)
+        top = v if parts else jnp.clip(v, -most, most)
+        top = top.astype(jnp.bfloat16).astype(F32)
         parts.append(top)
         v = v - top
     return parts
@@ -193,7 +195,7 @@
     xn = jnp.clip(x_prev - eta / omega * grad, 0.0, upper / scale)
     x_new[...] = xn
     v2 = scale * (xn - x_prev)
-    v1 = scale * xn + v2
+    v1 = 0.5 * (scale * xn) + 0.5 * v2
     sub = iota((up(2 * nbd, 8), bsz), 0)
     picks = []
     for k in range(nbd):
@@ -238,7 +240,7 @@
 
         both = lax.fori_loop(0, C, body, jnp.zeros((rb, bsz), F32), unroll=min(C, 8))
         scale = dr[at, :]
-        both = both * scale
+        both = both * (2.0 * scale)
         bs = scale * slot[base + rb : base + 2 * rb, :]
         yp = slot[base : base + rb, :]
         yn = yp + sigma * (bs - both)

time: 39.5 us -> 39.5 us (level)
  no operation moved by 1% of the time
where the time goes in v7:
time: 39.5 us; the launch traced here: 39.3 us
  blocking collectives  30.2 us (76%)
  Pallas kernels  4.14 us (10%)
  starting transfers between devices  3.12 us (8%)
  between operations  1.31 us (3%)
  waiting for transfers between devices  0.53 us (1%)
    all_to_all x3, blocking collectives, spread(): return lax.all_to_all(v, ('row', 'col'), 0, 0, tiled=True)  30.2 us
    ppermute x3, starting transfers between devices, swap(): return lax.ppermute(v, 'row', [(i, i ^ step) for i in range(R)])  3.12 us
    pallas_call x1, Pallas kernels, shards(): pl.pallas_call(functools.partial(peaks_kernel, nbd), out_shape=(shape(nde...  1.25 us
    pallas_call x1, Pallas kernels, shards(): pl.pallas_call(functools.partial(scales_kernel, *sizes), out_shape=(shape...  0.94 us
  transfers between devices with their start and end apart: 3, of which 1 were waited for; matrix products, arithmetic and copies ran while one was open for 0% of the time, Pallas kernels for 2%

profile of v7, /device:TPU:0, one launch (start us, length us, event | category | flops | bytes accessed | tf_op | source)
XLA Modules:
  0.0 39.3 jit_solution(8721703931353839110)
XLA Ops:
  1.3 1.2 %peaks.1 = (f32[32,1,640]{2,1,0:T(1,128)S(1)}, f32[576,128]{1,0:T(8,128)S(1)}, f32[32,128]{1,0:T(8,128)S(1)}, f32[512,128]{1,0:T(8,128)S(1)}) custom-call(f32[512,128]{1,0:T(8,128)} %bitcast.9, f32[32,128]{1,0:T(8,128)} %bitcast.10, f32[32,128]{1,0:T(8,128)} %bitcast.11, f32[8,128]{1,0:T(8,128)} %bitcast.12, f32[8,128]{1,0:T(8,128)} %bitcast.13, ...), custom_call_target="tpu_custom_call" | custom-call | tf_op jit(solution)/shard_map/peaks/pallas_call | solution.py:354
  2.5 3.0 %collective-permute-start.1 = (f32[576,128]{1,0:T(8,128)S(1)}, f32[576,128]{1,0:T(8,128)S(1)}, u32[]{:S(2)}, u32[]{:S(2)}) collective-permute-start(f32[576,128]{1,0:T(8,128)S(1)} %get-tuple-element.28.refs_0_), channel_id=1, source_target_pairs={{0,16},{8,24},{16,0},{24,8},{1,17},{9,25},{17,1},{25,9},{2,18},{10... | collective-permute-start | bytes 884744 | tf_op jit(solution)/shard_map/ppermute | solution.py:378
  5.5 0.0 collective-permute-start
  5.5 12.3 %all_to_all.15.g1 = f32[32,1,640]{2,1,0:T(1,128)S(1)} all-to-all(f32[32,1,640]{2,1,0:T(1,128)S(1)} %get-tuple-element.27), channel_id=1, replica_groups=mesh['row'=4,'col'=8] {'row','col'}, dimensions={0} | all-to-all | bytes 163840 | tf_op jit(solution)/shard_map/all_to_all | solution.py:375
  17.8 0.0 collective-permute-done.1.refs_2_
  17.8 0.0 collective-permute-done.refs_1_
  17.8 0.1 collective-permute-start.2
  17.9 0.9 %scales.1 = (f32[128,128]{1,0:T(8,128)S(1)}, f32[4,8,8,128]{3,2,1,0:T(8,128)S(1)}, f32[8,128]{1,0:T(8,128)S(1)}, f32[4,8,128]{2,1,0:T(8,128)S(1)}, f32[8,128]{1,...) custom-call(f32[32,1,640]{2,1,0:T(1,128)S(1)} %all_to_all.15.g1, ...), custom_call_target="tpu_custom_call" | custom-call | tf_op jit(solution)/shard_map/scales/pallas_call | solution.py:404
  18.9 0.5 %collective-permute-done.2.refs_0_.refs_3_ = f32[576,128]{1,0:T(8,128)S(1)} collective-permute-done((f32[576,128]{1,0:T(8,128)S(1)}, f32[576,128]{1,0:T(8,128)S(1)}, u32[]{:S(2)}, u32[]{:S(2)}) %collective-permute-start.2) | collective-permute-done | bytes 294944 | tf_op jit(solution)/shard_map/ppermute | solution.py:378
  19.4 0.6 %primal.1 = (f32[8,128]{1,0:T(8,128)S(1)}, f32[8,128]{1,0:T(8,128)S(1)}, f32[32,1,640]{2,1,0:T(1,128)S(1)}, bf16[1,3,512,128]{3,2,1,0:T(8,128)(2,1)S(1)}) custom-call(f32[576,128]{1,0:T(8,128)S(1)} %collective-permute-done.2.refs_0_.refs_3_, bf16[3,512,128]{2,1,0:T(8,128)(2,1)S(1)} %get-tuple-element.33.refs_1_, ...), custom_call_target="tpu_custom_call" | custom-call | tf_op jit(solution)/shard_map/primal/pallas_call | solution.py:421
  20.0 9.1 %all_to_all.16.g3 = f32[32,1,640]{2,1,0:T(1,128)S(1)} all-to-all(f32[32,1,640]{2,1,0:T(1,128)S(1)} %get-tuple-element.39), channel_id=1, replica_groups=mesh['row'=4,'col'=8] {'row','col'}, dimensions={0} | all-to-all | bytes 163840 | tf_op jit(solution)/shard_map/all_to_all | solution.py:375
  29.1 0.7 %dual.1 = (f32[32,128]{1,0:T(8,128)S(1)}, f32[32,1,128]{2,1,0:T(1,128)S(1)}, f32[8,128]{1,0:T(8,128)S(1)}) custom-call(f32[32,1,640]{2,1,0:T(1,128)S(1)} %all_to_all.16.g3, f32[576,128]{1,0:T(8,128)S(1)} %get-tuple-element.28.refs_0_, f32[576,128]{1,0:T(8,128)S(1)} %collective-permute-done.refs_1_, f32[576,128]{1,0:T(8,128)S(1)} %collective-permute-done.1.refs_2_, ...), custom_call_target="tpu_custom_call" | custom-call | tf_op jit(solution)/shard_map/dual/pallas_call | solution.py:436
  29.8 8.8 %all_to_all.17.g4 = f32[32,1,128]{2,1,0:T(1,128)S(1)} all-to-all(f32[32,1,128]{2,1,0:T(1,128)S(1)} %get-tuple-element.45), channel_id=1, replica_groups=mesh['row'=4,'col'=8] {'row','col'}, dimensions={0} | all-to-all | bytes 32768 | tf_op jit(solution)/shard_map/all_to_all | solution.py:375
  38.6 0.7 %stats.1 = (f32[1,3]{1,0:T(1,128)}, f32[8,128]{1,0:T(8,128)}, f32[32,128]{1,0:T(8,128)}) custom-call(f32[32,1,128]{2,1,0:T(1,128)S(1)} %all_to_all.17.g4, f32[8,128]{1,0:T(8,128)S(1)} %get-tuple-element.46.dual, f32[8,128]{1,0:T(8,128)S(1)} %get-tuple-element.43.refs_10_.x_new, f32[32,128]{1,0:T(8,128)S(1)} %get-tuple-element.47.y_new), custom_call_target="tpu_custom_call" | custom-call | tf_op jit(solution)/shard_map/stats/pallas_call | solution.py:446
Async XLA Ops:
  2.5 15.3 %collective-permute-start.1 = (f32[576,128]{1,0:T(8,128)S(1)}, f32[576,128]{1,0:T(8,128)S(1)}, u32[]{:S(2)}, u32[]{:S(2)}) collective-permute-start(f32[576,128]{1,0:T(8,128)S(1)} %get-tuple-element.28.refs_0_), channel_id=1, source_target_pairs={{0,16},{8,24},{16,0},{24,8},{1,17},{9,25},{17,1},{25,9},{2,18},{10... | collective-permute-start | bytes 884744 | tf_op jit(solution)/shard_map/ppermute | solution.py:378
  5.5 12.3 %collective-permute-start = (f32[576,128]{1,0:T(8,128)S(1)}, f32[576,128]{1,0:T(8,128)S(1)}, u32[]{:S(2)}, u32[]{:S(2)}) collective-permute-start(f32[576,128]{1,0:T(8,128)S(1)} %get-tuple-element.28.refs_0_), channel_id=1, source_target_pairs={{0,8},{8,0},{16,24},{24,16},{1,9},{9,1},{17,25},{25,17},{2,10},{10... | collective-permute-start | bytes 884744 | tf_op jit(solution)/shard_map/ppermute | solution.py:378
  17.8 1.6 %collective-permute-start.2 = (f32[576,128]{1,0:T(8,128)S(1)}, f32[576,128]{1,0:T(8,128)S(1)}, u32[]{:S(2)}, u32[]{:S(2)}) collective-permute-start(f32[576,128]{1,0:T(8,128)S(1)} %collective-permute-done.1.refs_2_), channel_id=1, source_target_pairs={{0,8},{8,0},{16,24},{24,16},{1,9},{9,1},{17,25},{25,17},{2,10},{10... | collective-permute-start | bytes 884744 | tf_op jit(solution)/shard_map/ppermute | solution.py:378

commit v8 on v7

--- a/solution.py
+++ b/solution.py
@@ -98,16 +98,20 @@
     return out
 
 
-def backward(nbd, rb, cb, q, parts, codes, w_ref):
+def pick(nbd, q, codes, values):
     me_c = lax.axis_index("col")
-    bsz = w_ref.shape[1]
-    rio = iota((rb, bsz), 0).astype(F32)
-    cio = iota((cb, bsz), 0).astype(F32)
-    w = w_ref[pl.ds(pl.multiple_of(q * rb, rb), rb), :]
-    picks = []
-    for k in range(nbd):
-        row = total(jnp.where(rio == codes[q, k, pl.ds(me_c, 1), :], w, 0.0))
-        picks.append(jnp.where(cio == codes[q, nbd + k, pl.ds(me_c, 1), :], row, 0.0))
+    rio = iota(values.shape, 0).astype(F32)
+    return [
+        total(jnp.where(rio == codes[q, k, pl.ds(me_c, 1), :], values, 0.0)) for k in range(nbd)
+    ]
+
+
+def backward(nbd, cb, q, parts, codes, rows):
+    me_c = lax.axis_index("col")
+    cio = iota((cb, rows[0].shape[1]), 0).astype(F32)
+    picks = [
+        jnp.where(cio == codes[q, nbd + k, pl.ds(me_c, 1), :], rows[k], 0.0) for k in range(nbd)
+    ]
     return product(jnp.concatenate(picks, axis=1), lambda i: parts[i], ((1,), (0,)))
 
 
@@ -159,7 +163,7 @@
     colmax[...] = top
     for s, (q, slot) in enumerate(zip(groups, slots)):
         split_blocks(nbd, slot, parts.at[s])
-        part[q] = backward(nbd, rb, cb, q, parts.at[s], codes, w_ref)
+        part[q] = backward(nbd, cb, q, parts.at[s], codes, pick(nbd, q, codes, w_ref[pl.ds(pl.multiple_of(q * rb, rb), rb), :]))
     split_blocks(nbd, turned, own)
 
 
@@ -185,7 +189,7 @@
         top = jnp.maximum(top, col_peaks(nbd, cb, q, slot, codes))
     for s, (q, slot) in enumerate(zip(groups, slots)):
         split_blocks(nbd, slot, parts.at[s])
-        part[q] = backward(nbd, rb, cb, q, parts.at[s], codes, w_ref)
+        part[q] = backward(nbd, cb, q, parts.at[s], codes, pick(nbd, q, codes, w_ref[pl.ds(pl.multiple_of(q * rb, rb), rb), :]))
     got = part[0]
     for q in range(1, R):
         got += part[q]
@@ -219,7 +223,7 @@
 
 def dual_kernel(nbd, R, C, rb, cb, origins, g3, *refs):
     slots = refs[:R]
-    early, late, aux, dr, codes, packed, x_new, dc, y_new, p4, dual, w_ref, part = refs[R:]
+    early, late, aux, dr, codes, packed, x_new, dc, y_new, p4, dual, part = refs[R:]
     me_r = lax.axis_index("row")
     me_c = lax.axis_index("col")
     bsz = x_new.shape[1]
@@ -228,34 +232,32 @@
     eta, omega = (aux[3 * cb + i : 3 * cb + i + 1, :] for i in range(2))
     rio = iota((rb, bsz), 0).astype(F32)
     sigma = eta * omega
+    half = early.shape[0]
     for s, slot in enumerate(slots):
         q = origins(me_r, s)
-        at = pl.ds(pl.multiple_of(q * rb, rb), rb)
-
-        def body(c, acc):
-            for k in range(nbd):
-                hit = rio == codes[q, k, pl.ds(c, 1), :]
-                acc = acc + jnp.where(hit, g3[q * C + c, :, k * bsz : (k + 1) * bsz], 0.0)
-            return acc
-
-        both = lax.fori_loop(0, C, body, jnp.zeros((rb, bsz), F32), unroll=min(C, 8))
-        scale = dr[at, :]
-        both = both * (2.0 * scale)
+        scale = dr[pl.ds(pl.multiple_of(q * rb, rb), rb), :]
         bs = scale * slot[base + rb : base + 2 * rb, :]
         yp = slot[base : base + rb, :]
-        yn = yp + sigma * (bs - both)
-        w_ref[at, :] = scale * yn
-        dy = yn - yp
-        part[q, 0:1, :] = total(dy * dy)
-        part[q, 1:2, :] = total(bs * yn)
         if s == 0:
-            y_new[...] = yn
+
+            def body(c, acc):
+                for k in range(nbd):
+                    hit = rio == codes[q, k, pl.ds(c, 1), :]
+                    acc = acc + jnp.where(hit, g3[q * C + c, :, k * bsz : (k + 1) * bsz], 0.0)
+                return acc
 
             def mine(c, acc):
                 hit = rio == packed[pl.ds(c, 1), :]
                 return acc + jnp.where(hit, g3[q * C + c, :, base:], 0.0)
 
-            shares = lax.fori_loop(0, C, mine, jnp.zeros((rb, bsz), F32), unroll=min(C, 8))
+            zero = jnp.zeros((rb, bsz), F32)
+            both = lax.fori_loop(0, C, body, zero, unroll=min(C, 8)) * (2.0 * scale)
+            shares = lax.fori_loop(0, C, mine, zero, unroll=min(C, 8))
+            yn = yp + sigma * (bs - both)
+            y_new[...] = yn
+            rows = pick(nbd, q, codes, scale * yn)
+            dy = yn - yp
+            dy2, by = total(dy * dy), total(bs * yn)
             lanes = bsz // C
             adx = shares
             for k in range(1, nbd):
@@ -264,18 +266,23 @@
             inside = iota((rb, bsz), 1) // lanes == C - 1 - me_c
             adx = jnp.where(inside, adx, 0.0)
             resid = jnp.where(inside, bs - (both - adx), 0.0)
-            adx2 = total(adx * adx)
-            res2 = total(resid * resid)
-    sums = part[0, :2, :]
-    for q in range(1, R):
-        sums += part[q, :2, :]
-    dual[:2, :] = jnp.broadcast_to(jnp.sum(sums, axis=1, keepdims=True), (2, bsz))
-    dual[2:, :] = jnp.broadcast_to(omega, (6, bsz))
-    groups = [origins(me_r, s) for s in range(R)]
-    half = early.shape[0]
-    for s, q in enumerate(groups):
+            adx2, res2 = total(adx * adx), total(resid * resid)
+        else:
+            at = pl.ds(q * C, C)
+            got = [g3[at, 0, k * bsz : (k + 1) * bsz] for k in range(nbd)]
+            still = pick(nbd, q, codes, yp + sigma * bs)
+            scales = pick(nbd, q, codes, scale)
+            rows = []
+            for k in range(nbd):
+                code = codes[q, k, pl.ds(me_c, 1), :]
+                both = jnp.zeros((C, bsz), F32)
+                for j in range(nbd):
+                    both = both + jnp.where(codes[q, j] == code, got[j], 0.0)
+                row = scales[k] * (still[k] - sigma * (total(both) * (2.0 * scales[k])))
+                rows.append(jnp.where(code >= 0.0, row, 0.0))
         parts = early.at[s] if s < half else late.at[s - half]
-        part[q] = backward(nbd, rb, cb, q, parts, codes, w_ref)
+        part[q] = backward(nbd, cb, q, parts, codes, rows)
+    dual[...] = jnp.broadcast_to(omega, dual.shape)
     got = part[0]
     for q in range(1, R):
         got += part[q]
@@ -285,7 +292,7 @@
     us = upper / scale
     xn = x_new[...]
     dx = xn - x_prev
-    terms = [total(dx * dx), total(cs * xn), total(us * jnp.maximum(-reduced, 0.0)), adx2, res2]
+    terms = [total(dx * dx), total(cs * xn), total(us * jnp.maximum(-reduced, 0.0)), adx2, res2, dy2, by]
     sub, lane = iota((8, bsz), 0), iota((8, bsz), 1)
     stack = jnp.zeros((8, bsz), F32)
     for i, term in enumerate(terms):
@@ -306,18 +313,20 @@
     sums = g4[0]
     for c in range(1, C):
         sums += g4[c]
+    groups = g4[0]
+    for q in range(1, g4.shape[0] // C):
+        groups += g4[q * C]
     every = sums
     for d in range(C, g4.shape[0]):
         every += g4[d]
     sub, lane = iota((8, bsz), 0), iota((8, bsz), 1)
-    stack = jnp.where(lane < 3, sums, every)
+    stack = jnp.where(lane < 3, sums, jnp.where(lane < 5, every, groups))
     stack = jnp.broadcast_to(
         jnp.sum(jnp.where(sub == lane, stack, 0.0), axis=1, keepdims=True), (8, bsz)
     )
-    dx2, cx, uneg, adx2, res2 = (stack[i : i + 1, :] for i in range(5))
-    dy2, by = (dual[i : i + 1, :] for i in range(2))
+    dx2, cx, uneg, adx2, res2, dy2, by = (stack[i : i + 1, :] for i in range(7))
     lane = lane[:1]
-    omega = dual[2:3, :]
+    omega = dual[:1, :]
     movement = 0.5 * omega * dx2 + 0.5 / omega * dy2
     first = jnp.sqrt(res2 / total_rows)
     second = (cx - by + uneg) / total_cols
@@ -438,7 +447,7 @@
         out_shape=(shape(rb, bsz), shape(ndev, 1, bsz), shape(8, bsz)),
         in_specs=[VMEM] * (R + 9),
         out_specs=(VMEM,) * 3,
-        scratch_shapes=scratch + [part],
+        scratch_shapes=[part],
         compiler_params=params,
         name="dual",
     )(g3, *slots, early, late, aux, dr, codes, packed, x_new, dc)

time: 39.5 us -> 39.4 us (level)
  no operation moved by 1% of the time
where the time goes in v8:
time: 39.4 us; the launch traced here: 39.2 us
  blocking collectives  30.2 us (77%)
  Pallas kernels  4.05 us (10%)
  starting transfers between devices  3.12 us (8%)
  between operations  1.31 us (3%)
  waiting for transfers between devices  0.53 us (1%)
    all_to_all x3, blocking collectives, spread(): return lax.all_to_all(v, ('row', 'col'), 0, 0, tiled=True)  30.2 us
    ppermute x3, starting transfers between devices, swap(): return lax.ppermute(v, 'row', [(i, i ^ step) for i in range(R)])  3.12 us
    pallas_call x1, Pallas kernels, shards(): pl.pallas_call(functools.partial(peaks_kernel, nbd), out_shape=(shape(nde...  1.25 us
    pallas_call x1, Pallas kernels, shards(): pl.pallas_call(functools.partial(scales_kernel, *sizes), out_shape=(shape...  0.94 us
  transfers between devices with their start and end apart: 3, of which 1 were waited for; matrix products, arithmetic and copies ran while one was open for 0% of the time, Pallas kernels for 2%

profile of v8, /device:TPU:0, one launch (start us, length us, event | category | flops | bytes accessed | tf_op | source)
XLA Modules:
  0.0 39.2 jit_solution(4373659531934668275)
XLA Ops:
  1.3 1.2 %peaks.1 = (f32[32,1,640]{2,1,0:T(1,128)S(1)}, f32[576,128]{1,0:T(8,128)S(1)}, f32[32,128]{1,0:T(8,128)S(1)}, f32[512,128]{1,0:T(8,128)S(1)}) custom-call(f32[512,128]{1,0:T(8,128)} %bitcast.9, f32[32,128]{1,0:T(8,128)} %bitcast.10, f32[32,128]{1,0:T(8,128)} %bitcast.11, f32[8,128]{1,0:T(8,128)} %bitcast.12, f32[8,128]{1,0:T(8,128)} %bitcast.13, ...), custom_call_target="tpu_custom_call" | custom-call | tf_op jit(solution)/shard_map/peaks/pallas_call | solution.py:363
  2.5 3.0 %collective-permute-start.1 = (f32[576,128]{1,0:T(8,128)S(1)}, f32[576,128]{1,0:T(8,128)S(1)}, u32[]{:S(2)}, u32[]{:S(2)}) collective-permute-start(f32[576,128]{1,0:T(8,128)S(1)} %get-tuple-element.28.refs_0_), channel_id=1, source_target_pairs={{0,16},{8,24},{16,0},{24,8},{1,17},{9,25},{17,1},{25,9},{2,18},{10... | collective-permute-start | bytes 884744 | tf_op jit(solution)/shard_map/ppermute | solution.py:387
  5.5 0.0 collective-permute-start
  5.5 12.3 %all_to_all.15.g1 = f32[32,1,640]{2,1,0:T(1,128)S(1)} all-to-all(f32[32,1,640]{2,1,0:T(1,128)S(1)} %get-tuple-element.27), channel_id=1, replica_groups=mesh['row'=4,'col'=8] {'row','col'}, dimensions={0} | all-to-all | bytes 163840 | tf_op jit(solution)/shard_map/all_to_all | solution.py:384
  17.8 0.0 collective-permute-done.1.refs_2_
  17.8 0.0 collective-permute-done.refs_1_
  17.8 0.1 collective-permute-start.2
  17.9 0.9 %scales.1 = (f32[128,128]{1,0:T(8,128)S(1)}, f32[4,8,8,128]{3,2,1,0:T(8,128)S(1)}, f32[8,128]{1,0:T(8,128)S(1)}, f32[4,8,128]{2,1,0:T(8,128)S(1)}, f32[8,128]{1,...) custom-call(f32[32,1,640]{2,1,0:T(1,128)S(1)} %all_to_all.15.g1, ...), custom_call_target="tpu_custom_call" | custom-call | tf_op jit(solution)/shard_map/scales/pallas_call | solution.py:413
  18.9 0.5 %collective-permute-done.2.refs_0_.refs_3_ = f32[576,128]{1,0:T(8,128)S(1)} collective-permute-done((f32[576,128]{1,0:T(8,128)S(1)}, f32[576,128]{1,0:T(8,128)S(1)}, u32[]{:S(2)}, u32[]{:S(2)}) %collective-permute-start.2) | collective-permute-done | bytes 294944 | tf_op jit(solution)/shard_map/ppermute | solution.py:387
  19.4 0.6 %primal.1 = (f32[8,128]{1,0:T(8,128)S(1)}, f32[8,128]{1,0:T(8,128)S(1)}, f32[32,1,640]{2,1,0:T(1,128)S(1)}, bf16[1,3,512,128]{3,2,1,0:T(8,128)(2,1)S(1)}) custom-call(f32[576,128]{1,0:T(8,128)S(1)} %collective-permute-done.2.refs_0_.refs_3_, bf16[3,512,128]{2,1,0:T(8,128)(2,1)S(1)} %get-tuple-element.33.refs_1_, ...), custom_call_target="tpu_custom_call" | custom-call | tf_op jit(solution)/shard_map/primal/pallas_call | solution.py:430
  20.0 9.1 %all_to_all.16.g3 = f32[32,1,640]{2,1,0:T(1,128)S(1)} all-to-all(f32[32,1,640]{2,1,0:T(1,128)S(1)} %get-tuple-element.39), channel_id=1, replica_groups=mesh['row'=4,'col'=8] {'row','col'}, dimensions={0} | all-to-all | bytes 163840 | tf_op jit(solution)/shard_map/all_to_all | solution.py:384
  29.1 0.6 %dual.1 = (f32[32,128]{1,0:T(8,128)S(1)}, f32[32,1,128]{2,1,0:T(1,128)S(1)}, f32[8,128]{1,0:T(8,128)S(1)}) custom-call(f32[32,1,640]{2,1,0:T(1,128)S(1)} %all_to_all.16.g3, f32[576,128]{1,0:T(8,128)S(1)} %get-tuple-element.28.refs_0_, f32[576,128]{1,0:T(8,128)S(1)} %collective-permute-done.refs_1_, f32[576,128]{1,0:T(8,128)S(1)} %collective-permute-done.1.refs_2_, ...), custom_call_target="tpu_custom_call" | custom-call | tf_op jit(solution)/shard_map/dual/pallas_call | solution.py:445
  29.7 8.8 %all_to_all.17.g4 = f32[32,1,128]{2,1,0:T(1,128)S(1)} all-to-all(f32[32,1,128]{2,1,0:T(1,128)S(1)} %get-tuple-element.45), channel_id=1, replica_groups=mesh['row'=4,'col'=8] {'row','col'}, dimensions={0} | all-to-all | bytes 32768 | tf_op jit(solution)/shard_map/all_to_all | solution.py:384
  38.6 0.7 %stats.1 = (f32[1,3]{1,0:T(1,128)}, f32[8,128]{1,0:T(8,128)}, f32[32,128]{1,0:T(8,128)}) custom-call(f32[32,1,128]{2,1,0:T(1,128)S(1)} %all_to_all.17.g4, f32[8,128]{1,0:T(8,128)S(1)} %get-tuple-element.46.dual, f32[8,128]{1,0:T(8,128)S(1)} %get-tuple-element.43.refs_10_.x_new, f32[32,128]{1,0:T(8,128)S(1)} %get-tuple-element.47.y_new), custom_call_target="tpu_custom_call" | custom-call | tf_op jit(solution)/shard_map/stats/pallas_call | solution.py:455
Async XLA Ops:
  2.5 15.3 %collective-permute-start.1 = (f32[576,128]{1,0:T(8,128)S(1)}, f32[576,128]{1,0:T(8,128)S(1)}, u32[]{:S(2)}, u32[]{:S(2)}) collective-permute-start(f32[576,128]{1,0:T(8,128)S(1)} %get-tuple-element.28.refs_0_), channel_id=1, source_target_pairs={{0,16},{8,24},{16,0},{24,8},{1,17},{9,25},{17,1},{25,9},{2,18},{10... | collective-permute-start | bytes 884744 | tf_op jit(solution)/shard_map/ppermute | solution.py:387
  5.5 12.3 %collective-permute-start = (f32[576,128]{1,0:T(8,128)S(1)}, f32[576,128]{1,0:T(8,128)S(1)}, u32[]{:S(2)}, u32[]{:S(2)}) collective-permute-start(f32[576,128]{1,0:T(8,128)S(1)} %get-tuple-element.28.refs_0_), channel_id=1, source_target_pairs={{0,8},{8,0},{16,24},{24,16},{1,9},{9,1},{17,25},{25,17},{2,10},{10... | collective-permute-start | bytes 884744 | tf_op jit(solution)/shard_map/ppermute | solution.py:387
  17.8 1.6 %collective-permute-start.2 = (f32[576,128]{1,0:T(8,128)S(1)}, f32[576,128]{1,0:T(8,128)S(1)}, u32[]{:S(2)}, u32[]{:S(2)}) collective-permute-start(f32[576,128]{1,0:T(8,128)S(1)} %collective-permute-done.1.refs_2_), channel_id=1, source_target_pairs={{0,8},{8,0},{16,24},{24,16},{1,9},{9,1},{17,25},{25,17},{2,10},{10... | collective-permute-start | bytes 884744 | tf_op jit(solution)/shard_map/ppermute | solution.py:387
